TPU v7x, 256 devices: a whole 4x4x8 slice. The times are simulated.
256 devices in a mesh: band: 64 (over z, y, core), lev: 4 (over x).
Axes of the slice: x: 4, y: 4, z: 8, core: 2. Of those that a mesh axis runs over, the one named last changes fastest.
Arguments:
- winds: float32 [3, 4, 2097152], P(None, 'lev', 'band'), may hold values from -6 to 6
- remap_w: float32 [4, 64, 4096], P(None, 'band'), may hold values from 0.1 to 1
- remap_col: int32 [4, 64, 4096], P(None, 'band'), may hold values from 0 to 1535
- block_pick: int32 [64, 768], replicated, may hold values from 0 to 255
- cycle_ids: int32 [64], P('band'), may hold values from 1024 to 3072
- wave_ids: int32 [2048], replicated, may hold values from 0 to 2047, each once
- legendre_a: bfloat16 [2048, 64, 2048], P(('band', 'lev')), may hold values from -0.01171875 to 0.01171875
- legendre_b: bfloat16 [2048, 64, 2048], P(('band', 'lev')), may hold values from -0.01171875 to 0.01171875
Outputs:
- divergence: float32 [2, 4, 2048, 2048], P(None, None, ('band', 'lev'))
- vorticity: float32 [2, 4, 2048, 2048], P(None, None, ('band', 'lev'))
Inputs may be any that keep to these rules, and one draw needn't show every extreme that they name: `block_pick`: block indices within one column shard. `remap_col`: offsets within the 12 picked blocks of one source column shard. `cycle_ids`: Equatorial-belt cycle numbers. `wave_ids`: each wavenumber below 2048 once.
All inputs are finite; a program needn't handle non-finite values.
Results may differ from a plain program's by a relative error of at most 0.0029.
Values may be sent and summed in bfloat16 or wider, within the bound.
A program may use at most 192 MiB of HBM per device.

v0:
```python
import math

import jax
import jax.numpy as jnp
from jax import lax
from jax.sharding import PartitionSpec as P

NSIDE = 1024
M = 2048
BLK = 128
PER = 12


HIGHEST = lax.Precision.HIGHEST


def geometry(cycle_number, nside):
    cycle_float = cycle_number.astype(jnp.float32)
    cos_theta = 4.0 / 3.0 - 2.0 * cycle_float / (3.0 * nside)
    sin_theta = jnp.sqrt(1.0 - cos_theta * cos_theta)
    half_shift = ((cycle_number - nside + 1) % 2).astype(jnp.float32)
    return (cos_theta, sin_theta, half_shift)


def cycle_spectrum(samples, waves):
    row_count, cycle_length = samples.shape
    outer = 64
    inner = cycle_length // outer
    grid = samples.reshape(row_count, outer, inner)
    first_k = jnp.arange(outer, dtype=jnp.int32)
    inner_n = jnp.arange(inner, dtype=jnp.int32)
    angle_one = (
        2.0 * math.pi / outer * (first_k[:, None] * first_k[None, :] % outer).astype(jnp.float32)
    )
    section_real = jnp.einsum("ka,rab->rkb", jnp.cos(angle_one), grid, precision=HIGHEST)
    section_imag = -jnp.einsum("ka,rab->rkb", jnp.sin(angle_one), grid, precision=HIGHEST)
    angle_two = (
        2.0
        * math.pi
        / cycle_length
        * (first_k[:, None] * inner_n[None, :] % cycle_length).astype(jnp.float32)
    )
    twist_cos = jnp.cos(angle_two)[None]
    twist_sin = jnp.sin(angle_two)[None]
    turned_real = section_real * twist_cos + section_imag * twist_sin
    turned_imag = section_imag * twist_cos - section_real * twist_sin
    second_k = jnp.arange(waves // outer, dtype=jnp.int32)
    angle_three = (
        2.0 * math.pi / inner * (inner_n[:, None] * second_k[None, :] % inner).astype(jnp.float32)
    )
    cos_three = jnp.cos(angle_three)
    sin_three = jnp.sin(angle_three)
    out_real = jnp.einsum("rkb,bq->rqk", turned_real, cos_three, precision=HIGHEST) + jnp.einsum(
        "rkb,bq->rqk", turned_imag, sin_three, precision=HIGHEST
    )
    out_imag = jnp.einsum("rkb,bq->rqk", turned_imag, cos_three, precision=HIGHEST) - jnp.einsum(
        "rkb,bq->rqk", turned_real, sin_three, precision=HIGHEST
    )
    return (out_real.reshape(row_count, waves), out_imag.reshape(row_count, waves))


def select_waves(modes, order):
    lead = modes.shape[:3]
    wave_count = modes.shape[3]
    selector = (jnp.arange(wave_count, dtype=jnp.int32)[:, None] == order[None, :]).astype(
        jnp.bfloat16
    )
    flat = modes.reshape(-1, wave_count)
    picked = jnp.dot(flat, selector, preferred_element_type=jnp.float32).astype(jnp.bfloat16)
    return picked.reshape(lead + (order.shape[0],))


def local(winds, remap_w, remap_col, block_pick, cycle_ids, wave_ids, legendre_a, legendre_b):
    band_count = lax.axis_size("band")
    level_count = lax.axis_size("lev")
    band_index = lax.axis_index("band")
    level_index = lax.axis_index("lev")
    components, levels_dev, column_count = winds.shape
    tap_count, cycle_count, cycle_length = remap_col.shape
    pixel_count = cycle_count * cycle_length
    pixel_ids = jnp.arange(pixel_count, dtype=jnp.int32)
    source = pixel_ids % band_count
    col_flat = remap_col.reshape(tap_count, pixel_count)
    weights = remap_w.reshape(tap_count, pixel_count)
    mine_picks = lax.dynamic_slice_in_dim(block_pick, band_index * PER, PER, 1)
    blocks = winds.reshape(components, levels_dev, column_count // BLK, BLK)
    chosen = jnp.take(blocks, mine_picks.reshape(-1), axis=2)
    outgoing = chosen.reshape(components, levels_dev, band_count, PER * BLK)
    received = lax.all_to_all(outgoing, "band", split_axis=2, concat_axis=2, tiled=True)
    flattened = received.reshape(components, levels_dev, band_count * PER * BLK)
    tap_index = source[None, :] * (PER * BLK) + col_flat
    sampled = jnp.take(flattened, tap_index.reshape(-1), axis=2).reshape(
        components, levels_dev, tap_count, pixel_count
    )
    cartesian_flat = jnp.sum(sampled * weights[None, None], axis=2)
    cartesian = cartesian_flat.reshape(components, levels_dev, cycle_count, cycle_length)
    cos_theta, sin_theta, half_shift = geometry(cycle_ids, NSIDE)
    spacing = math.pi / (2.0 * NSIDE)
    position = jnp.arange(cycle_length, dtype=jnp.int32)[None, :]
    azimuth = spacing * (position.astype(jnp.float32) + 1.0 - 0.5 * half_shift[:, None])
    cos_phi = jnp.cos(azimuth)
    sin_phi = jnp.sin(azimuth)
    east = -sin_phi * cartesian[0] + cos_phi * cartesian[1]
    north = (
        -cos_theta[:, None] * (cos_phi * cartesian[0] + sin_phi * cartesian[1])
        + sin_theta[:, None] * cartesian[2]
    )
    stacked = jnp.stack([east, north]).reshape(2 * levels_dev * cycle_count, cycle_length)
    raw_real, raw_imag = cycle_spectrum(stacked, M)
    raw_real = raw_real.reshape(2, levels_dev, cycle_count, M)
    raw_imag = raw_imag.reshape(2, levels_dev, cycle_count, M)
    start = spacing * (1.0 - 0.5 * half_shift)
    angle = start[:, None] * jnp.arange(M, dtype=jnp.int32).astype(jnp.float32)[None, :]
    cos_rot = jnp.cos(angle)
    sin_rot = jnp.sin(angle)
    rot_real = raw_real * cos_rot + raw_imag * sin_rot
    rot_imag = raw_imag * cos_rot - raw_real * sin_rot
    modes = jnp.stack([rot_real[0], rot_imag[0], rot_real[1], rot_imag[1]], axis=1).astype(
        jnp.bfloat16
    )
    owned = M // (band_count * level_count)
    outgoing_modes = select_waves(modes, wave_ids)
    gathered = lax.all_to_all(
        lax.all_to_all(outgoing_modes, "band", split_axis=3, concat_axis=2, tiled=True),
        "lev",
        split_axis=3,
        concat_axis=0,
        tiled=True,
    )
    all_levels = gathered.shape[0]
    all_cycles = gathered.shape[2]
    mode_rows = jnp.transpose(gathered, (3, 0, 1, 2)).reshape(owned, all_levels * 4, all_cycles)
    dims = (((2,), (1,)), ((0,), (0,)))
    part_a = lax.dot_general(mode_rows, legendre_a, dims, preferred_element_type=jnp.float32)
    part_b = lax.dot_general(mode_rows, legendre_b, dims, preferred_element_type=jnp.float32)
    degrees = part_a.shape[2]
    part_a = part_a.reshape(owned, all_levels, 4, degrees)
    part_b = part_b.reshape(owned, all_levels, 4, degrees)
    slot_start = (band_index * level_count + level_index) * owned
    my_waves = lax.dynamic_slice_in_dim(wave_ids, slot_start, owned)
    upper = (jnp.arange(degrees, dtype=jnp.int32)[None, :] >= my_waves[:, None])[:, None, :]
    div_real = jnp.where(upper, -part_a[:, :, 1] - part_b[:, :, 2], 0.0)
    div_imag = jnp.where(upper, part_a[:, :, 0] - part_b[:, :, 3], 0.0)
    vort_real = jnp.where(upper, -part_a[:, :, 3] + part_b[:, :, 0], 0.0)
    vort_imag = jnp.where(upper, part_a[:, :, 2] + part_b[:, :, 1], 0.0)
    divergence = jnp.transpose(jnp.stack([div_real, div_imag]), (0, 2, 1, 3))
    vorticity = jnp.transpose(jnp.stack([vort_real, vort_imag]), (0, 2, 1, 3))
    return (divergence, vorticity)


def solution(mesh):
    placed = (
        P(None, "lev", "band"),
        P(None, "band", None),
        P(None, "band", None),
        P(),
        P("band"),
        P(),
        P(("band", "lev"), None, None),
        P(("band", "lev"), None, None),
    )
    return jax.shard_map(
        local,
        mesh=mesh,
        in_specs=placed,
        out_specs=(P(None, None, ("band", "lev"), None), P(None, None, ("band", "lev"), None)),
        check_vma=False,
    )
```

profile of v0, /device:TPU:1, one launch (start us, length us, event | category | flops | bytes accessed | tf_op | source)
XLA Modules:
  0.0 227.3 jit_solution(4185967276356496594)
XLA Ops:
  0.6 1.4 copy.99
  2.1 0.9 compare_and_fusion.1
  3.0 0.1 reshape.636
  3.1 3.4 %gather_fusion = f32[768,3,128]{2,1,0:T(4,128)} fusion(f32[3,256,128]{2,0,1:T(4,128)S(1)} %copy.99, s32[1024]{0:T(1024)S(1)} %pad_clamp_fusion), kind=kCustom, calls=%fused_computation | custom fusion | bytes 2362368 | tf_op jit(solution)/shard_map/jit(_take)/gather | solution.py:87
  6.6 2.5 %copy.100 = f32[3,768,128]{2,1,0:T(8,128)} copy(f32[3,768,128]{2,0,1:T(4,128)} %bitcast.104) | data formatting | bytes 2359296 | tf_op jit(solution)/shard_map/jit(_take)/gather | solution.py:87
  9.1 1.5 gather.13
  10.6 0.2 broadcast_in_dim.78
  10.8 0.1 broadcast_select_fusion
  11.0 2.2 copy.101
  13.2 13.2 %all-to-all-start = ((f32[3,1,64,1536]{3,1,0,2:T(1,128)}), f32[3,1,64,1536]{3,1,0,2:T(1,128)S(1)}, u32[]{:S(2)}, u32[]{:S(2)}) async-start(f32[3,1,64,1536]{3,1,0,2:T(1,128)} %copy.101), calls=%async_computation | async-start | bytes 2359296 | tf_op jit(solution)/shard_map/all_to_all | solution.py:89
  26.5 0.1 compare_select_fusion
  27.3 0.9 copy.178
  28.2 0.1 fusion.50
  28.4 0.8 fusion.51
  29.2 0.8 copy.108
  30.0 0.7 fusion.60
  30.7 0.6 broadcast_clamp_fusion
  31.4 25.5 %all-to-all-done = f32[3,1,64,1536]{3,1,0,2:T(1,128)S(1)} async-done(((f32[3,1,64,1536]{3,1,0,2:T(1,128)}), f32[3,1,64,1536]{3,1,0,2:T(1,128)S(1)}, u32[]{:S(2)}, u32[]{:S(2)}) %all-to-all-start) | async-done | bytes 1179680 | tf_op jit(solution)/shard_map/all_to_all | solution.py:89
  57.0 23.8 %copy.102 = f32[3,1,64,1536]{0,3,2,1:T(8,128)} copy(f32[3,1,64,1536]{3,1,0,2:T(1,128)S(1)} %all-to-all-done) | data formatting | bytes 2359296 | tf_op jit(solution)/shard_map/all_to_all | solution.py:89
  80.7 69.8 %gather_fusion.1 = f32[16384,3]{1,0:T(8,128)} fusion(f32[3,98304]{0,1:T(8,128)} %bitcast.102, s32[16384]{0:T(1024)S(1)} %copy-done.6), kind=kCustom, calls=%fused_computation.1 | custom fusion | bytes 458752 | tf_op jit(solution)/shard_map/jit(_take)/gather | solution.py:92
  150.5 6.9 %multiply_reduce_fusion = f32[3,4096]{0,1:T(8,128)S(1)} fusion(f32[3,1,4,4096]{0,3,2,1:T(8,128)} %bitcast.103, f32[4,4096]{1,0:T(4,128)S(1)} %bitcast.110, pred[4,4096]{1,0:T(4,128)(4,1)S(1)} %compare_and_fusion), kind=kLoop, calls=%fused_computation.5 | loop fusion | flops 135168 | bytes 327680 | tf_op jit(solution)/shard_map/reduce_sum | solution.py:95
  157.5 2.8 %slice_reduce_fusion.1 = (f32[4096]{0:T(1024)S(1)}, f32[4096]{0:T(1024)S(1)}, f32[4096]{0:T(1024)S(1)}) fusion(f32[3,4096]{0,1:T(8,128)S(1)} %multiply_reduce_fusion, f32[]{:T(128)} %bitcast.10), kind=kLoop, calls=%fused_computation.11 | loop fusion | flops 4096 | bytes 98308 | tf_op jit(solution)/shard_map/slice | solution.py:103
  160.7 0.2 multiply_add_fusion.2
  160.9 0.3 convolution_bitcast_fusion
  161.2 0.3 fusion.5
  161.6 0.2 fusion.46
  161.8 0.3 fusion.48
  162.1 0.3 fusion.6
  162.4 0.2 fusion.7
  162.9 3.0 %fusion.3 = bf16[1,4,1,2048]{3,1,2,0:T(4,128)(2,1)S(1)} fusion(s32[2048]{0:T(1024)S(1)} %copy-done.9, bf16[1,2048]{1,0:T(2,128)(2,1)S(1)} %get-tuple-element.26, bf16[1,2048]{1,0:T(2,128)(2,1)S(1)} %get-tuple-element.24, bf16[1,2048]{1,0:T(2,128)(2,1)S(1)} %get-tuple-element.25, bf16[1,2048]{1,0:T(2,128)(2,1)S(1)} %get-tuple-element.23), kind=kOutput, calls=%fused_computation.7 | convolution fusion | flops 37822464 | bytes 40960 | tf_op jit(solution)/shard_map/dot_general | solution.py:69
  165.9 2.0 copy.114
  167.9 6.6 %all-to-all-start.1 = ((bf16[1,4,1,2048]{1,2,0,3:T(2,128)(2,1)}), bf16[1,4,1,2048]{1,2,0,3:T(2,128)(2,1)S(1)}, u32[]{:S(2)}, u32[]{:S(2)}) async-start(bf16[1,4,1,2048]{1,2,0,3:T(2,128)(2,1)} %copy.114), calls=%async_computation.1 | async-start | bytes 2097152 | tf_op jit(solution)/shard_map/all_to_all | solution.py:124
  174.7 27.9 %all-to-all-done.1 = bf16[1,4,1,2048]{1,2,0,3:T(2,128)(2,1)S(1)} async-done(((bf16[1,4,1,2048]{1,2,0,3:T(2,128)(2,1)}), bf16[1,4,1,2048]{1,2,0,3:T(2,128)(2,1)S(1)}, u32[]{:S(2)}, u32[]{:S(2)}) %all-to-all-start.1) | async-done | bytes 16416 | tf_op jit(solution)/shard_map/all_to_all | solution.py:124
  202.6 0.6 copy.115
  203.1 0.1 all_to_all.27
  203.3 0.1 copy.116
  203.4 0.7 reshape.675
  204.1 4.0 %all-to-all-start.2 = ((bf16[4,2,1024]{2,1,0:T(2,128)(2,1)}), bf16[4,2,1024]{2,1,0:T(2,128)(2,1)S(1)}, u32[]{:S(2)}, u32[]{:S(2)}) async-start(bf16[4,2,1024]{2,1,0:T(2,128)(2,1)} %reshape.675), calls=%async_computation.2 | async-start | bytes 32768 | tf_op jit(solution)/shard_map/all_to_all | solution.py:123
  208.2 4.1 %all-to-all-done.2 = bf16[4,2,1024]{2,1,0:T(2,128)(2,1)S(1)} async-done(((bf16[4,2,1024]{2,1,0:T(2,128)(2,1)}), bf16[4,2,1024]{2,1,0:T(2,128)(2,1)S(1)}, u32[]{:S(2)}, u32[]{:S(2)}) %all-to-all-start.2) | async-done | bytes 16416 | tf_op jit(solution)/shard_map/all_to_all | solution.py:123
  212.5 0.4 fusion.99
  212.9 1.3 reshape.642
  214.1 4.5 %fusion.97 = (f32[8,4,1,2048]{3,2,1,0:T(1,128)S(1)}, f32[8,4,1,2048]{3,2,1,0:T(1,128)}, f32[8,4,1,2048]{3,2,1,0:T(1,128)}, f32[8,4,1,2048]{3,2,1,0:T(1,128)}) fusion(f32[8,4,4,2048]{3,2,1,0:T(4,128)} %reshape.642), kind=kLoop, calls=%fused_computation.150 | loop fusion | bytes 2097152 | tf_op jit(solution)/shard_map/slice | solution.py:144
  218.6 0.4 fusion.98
  219.0 1.3 reshape.641
  220.3 3.6 %fusion.96 = (f32[8,4,1,2048]{3,2,1,0:T(1,128)S(1)}, f32[8,4,1,2048]{3,2,1,0:T(1,128)S(1)}, f32[8,4,1,2048]{3,2,1,0:T(1,128)S(1)}, f32[8,4,1,2048]{3,2,1,0:T(1,128)S(1)}) fusion(f32[8,4,4,2048]{3,2,1,0:T(4,128)} %reshape.641), kind=kLoop, calls=%fused_computation.149 | loop fusion | bytes 2097152 | tf_op jit(solution)/shard_map/slice | solution.py:144
  224.0 1.6 fusion.11
  225.6 0.8 maximum_bitcast_fusion
  226.4 0.8 maximum_bitcast_fusion.1
  (44 shorter events, 1.3 us)
Async XLA Ops:
  0.6 211.8 %copy-start = (bf16[8,64,2048]{2,1,0:T(8,128)(2,1)S(1)}, bf16[8,64,2048]{2,1,0:T(8,128)(2,1)}, u32[]{:S(2)}) copy-start(bf16[8,64,2048]{2,1,0:T(8,128)(2,1)} %param.15) | copy-start | bytes 6291460
  10.9 15.5 %copy-start.5 = (s32[4,1,4096]{2,1,0:T(1,128)S(1)}, s32[4,1,4096]{2,1,0:T(1,128)}, u32[]{:S(2)}) copy-start(s32[4,1,4096]{2,1,0:T(1,128)} %param.10) | copy-start | bytes 196612
  13.2 43.8 %all-to-all-start = ((f32[3,1,64,1536]{3,1,0,2:T(1,128)}), f32[3,1,64,1536]{3,1,0,2:T(1,128)S(1)}, u32[]{:S(2)}, u32[]{:S(2)}) async-start(f32[3,1,64,1536]{3,1,0,2:T(1,128)} %copy.101), calls=%async_computation | async-start | bytes 2359296 | tf_op jit(solution)/shard_map/all_to_all | solution.py:89
  31.4 49.3 %copy-start.6 = (s32[16384]{0:T(1024)S(1)}, s32[16384]{0:T(1024)}, u32[]{:S(2)}) copy-start(s32[16384]{0:T(1024)} %broadcast_clamp_fusion) | copy-start | bytes 196612
  157.4 5.3 %copy-start.7 = (f32[2048]{0:T(1024)S(1)}, f32[2048]{0:T(1024)}, u32[]{:S(2)}) copy-start(f32[2048]{0:T(1024)} %get-tuple-element.27) | copy-start | bytes 24580
  157.4 5.3 %copy-start.8 = (f32[2048]{0:T(1024)S(1)}, f32[2048]{0:T(1024)}, u32[]{:S(2)}) copy-start(f32[2048]{0:T(1024)} %get-tuple-element.28) | copy-start | bytes 24580
  160.3 2.6 %copy-start.9 = (s32[2048]{0:T(1024)S(1)}, s32[2048]{0:T(1024)}, u32[]{:S(2)}) copy-start(s32[2048]{0:T(1024)} %param.13) | copy-start | bytes 24580
  167.9 34.6 %all-to-all-start.1 = ((bf16[1,4,1,2048]{1,2,0,3:T(2,128)(2,1)}), bf16[1,4,1,2048]{1,2,0,3:T(2,128)(2,1)S(1)}, u32[]{:S(2)}, u32[]{:S(2)}) async-start(bf16[1,4,1,2048]{1,2,0,3:T(2,128)(2,1)} %copy.114), calls=%async_computation.1 | async-start | bytes 2097152 | tf_op jit(solution)/shard_map/all_to_all | solution.py:124
  204.1 8.2 %all-to-all-start.2 = ((bf16[4,2,1024]{2,1,0:T(2,128)(2,1)}), bf16[4,2,1024]{2,1,0:T(2,128)(2,1)S(1)}, u32[]{:S(2)}, u32[]{:S(2)}) async-start(bf16[4,2,1024]{2,1,0:T(2,128)(2,1)} %reshape.675), calls=%async_computation.2 | async-start | bytes 32768 | tf_op jit(solution)/shard_map/all_to_all | solution.py:123
  214.1 4.5 %copy-start.1 = (bf16[8,64,2048]{2,1,0:T(8,128)(2,1)S(1)}, bf16[8,64,2048]{2,1,0:T(8,128)(2,1)}, u32[]{:S(2)}) copy-start(bf16[8,64,2048]{2,1,0:T(8,128)(2,1)} %param.14) | copy-start | bytes 6291460
  220.3 3.7 %copy-start.2 = (f32[8,4,1,2048]{3,2,1,0:T(1,128)S(1)}, f32[8,4,1,2048]{3,2,1,0:T(1,128)}, u32[]{:S(2)}) copy-start(f32[8,4,1,2048]{3,2,1,0:T(1,128)} %get-tuple-element.12) | copy-start | bytes 786436
  220.3 3.7 %copy-start.3 = (f32[8,4,1,2048]{3,2,1,0:T(1,128)S(1)}, f32[8,4,1,2048]{3,2,1,0:T(1,128)}, u32[]{:S(2)}) copy-start(f32[8,4,1,2048]{3,2,1,0:T(1,128)} %get-tuple-element.13) | copy-start | bytes 786436
  220.3 3.7 %copy-start.4 = (f32[8,4,1,2048]{3,2,1,0:T(1,128)S(1)}, f32[8,4,1,2048]{3,2,1,0:T(1,128)}, u32[]{:S(2)}) copy-start(f32[8,4,1,2048]{3,2,1,0:T(1,128)} %get-tuple-element.14) | copy-start | bytes 786436
where the time goes:
time: 229 us; the launch traced here: 227 us
  local copies, waits for them, and re-layouts  122 us (53%)
  waiting for transfers between devices  57.6 us (25%)
  starting transfers between devices  23.8 us (10%)
  other arithmetic  16.7 us (7%)
  matrix products  5.48 us (2%)
    gather x1, local copies, waits for them, and re-layouts, local(): jnp.take(flattened, tap_index.reshape(-1), axis=2)  69.8 us
    all_to_all x1, waiting for transfers between devices, local(): lax.all_to_all(outgoing_modes, 'band', split_axis=3, concat_axis=2, tiled...  27.9 us
    all_to_all x1, waiting for transfers between devices, local(): lax.all_to_all(outgoing, 'band', split_axis=2, concat_axis=2, tiled=True)  25.5 us
    all_to_all x1, local copies, waits for them, and re-layouts, local(): lax.all_to_all(outgoing, 'band', split_axis=2, concat_axis=2, tiled=True)  23.8 us
    all_to_all x1, starting transfers between devices, local(): lax.all_to_all(outgoing, 'band', split_axis=2, concat_axis=2, tiled=True)  13.2 us
    slice x2, local copies, waits for them, and re-layouts, local(): vort_real = jnp.where(upper, -part_a[:, :, 3] + part_b[:, :, 0], 0.0)  8.1 us
    gather x3, local copies, waits for them, and re-layouts, local(): chosen = jnp.take(blocks, mine_picks.reshape(-1), axis=2)  7.41 us
    reduce_sum x1, other arithmetic, local(): cartesian_flat = jnp.sum(sampled * weights[None, None], axis=2)  6.93 us
  transfers between devices with their start and end apart: 3, of which 3 were waited for; matrix products, arithmetic and copies ran while one was open for 2% of the time, Pallas kernels for 0%

commit v1 on v0

v1 whole, which is shorter than its diff:
```python
import functools
import math

import jax
import jax.numpy as jnp
import numpy as np
from jax import lax
from jax.experimental import pallas as pl
from jax.experimental.pallas import tpu as pltpu
from jax.sharding import PartitionSpec as P

NSIDE = 1024
NPHI = 4096
M = 2048
BLK = 128
PER = 12
TAPS = 4
LANES = 128

f32 = jnp.float32
bf16 = jnp.bfloat16


def split(table):
    table = np.asarray(table, np.float32)
    high = table.astype(jnp.bfloat16)
    low = (table - high.astype(np.float32)).astype(jnp.bfloat16)
    return high, low


@functools.cache
def tables(band):
    rho = np.arange(2 * band)
    n = (rho % 2) * band + rho // 2
    b = np.arange(NPHI // (2 * band))
    mu = np.arange(LANES)
    m1 = np.arange(M // LANES)
    turn = 2.0 * np.pi / NPHI
    coef, twiddle, outer_hi, outer_lo = [], [], [], []
    for half in (0, 1):
        delta = 1.0 - 0.5 * half
        azimuth = turn * (2 * band * b[None, :] + n[:, None] + delta)
        zero = np.zeros_like(azimuth)
        cos, sin = np.cos(azimuth), np.sin(azimuth)
        coef.append(np.stack([np.concatenate([-sin, cos, zero, zero], 1), np.concatenate([cos, sin, zero, zero], 1)]))
        phi = turn * mu[None, :] * (n[:, None] + delta)
        twiddle.append(np.stack([np.cos(phi), np.sin(phi)]))
        psi = turn * LANES * m1[:, None] * (n[None, :] + delta)
        full = np.concatenate(
            [np.concatenate([np.cos(psi), np.sin(psi)], 1), np.concatenate([-np.sin(psi), np.cos(psi)], 1)], 0
        )
        high, low = split(full)
        outer_hi.append(high)
        outer_lo.append(low)
    angle = 2.0 * np.pi / b.size * (b[:, None] * mu[None, :])
    inner = np.tile(np.concatenate([np.cos(angle), -np.sin(angle)], 1), (4, 1))
    inner_hi, inner_lo = split(inner)
    return (
        np.stack(coef).astype(np.float32),
        np.stack(twiddle).astype(np.float32),
        np.stack([inner_hi, inner_lo]),
        np.stack([np.stack(outer_hi), np.stack(outer_lo)]),
    )


def dot(a, b):
    return jnp.dot(a, b, preferred_element_type=f32)


def high_low(x):
    high = x.astype(bf16)
    return high, (x - high.astype(f32)).astype(bf16)


def take(x, index):
    return jnp.take_along_axis(x, index, axis=1, mode="promise_in_bounds")


def modes_kernel(
    band,
    lev,
    cycle_ref,
    winds_hbm,
    weight_hbm,
    column_hbm,
    pick_hbm,
    wave_hbm,
    coef_hbm,
    twiddle_hbm,
    inner_hbm,
    outer_hbm,
    out_ref,
    winds,
    weight,
    column,
    pick,
    wave,
    coef,
    twiddle,
    inner,
    outer,
    table,
    request_out,
    request_in,
    reply_out,
    reply_in,
    spectrum,
    rows_out,
    rows_in,
    turned,
    levels_in,
    local_sem,
    send_sem,
    recv_sem,
):
    me = lax.axis_index("band")
    my_lev = lax.axis_index("lev")
    window = jnp.minimum(me * PER // LANES, PER * band // LANES - 2)
    pick_at = me * PER - window * LANES
    loads = [
        pltpu.make_async_copy(source, target, local_sem.at[i])
        for i, (source, target) in enumerate(
            (
                (column_hbm, column),
                (weight_hbm, weight),
                (winds_hbm, winds),
                (pick_hbm.at[:, pl.ds(pl.multiple_of(window * LANES, LANES), 2 * LANES)], pick),
                (coef_hbm, coef),
                (twiddle_hbm, twiddle),
                (inner_hbm, inner),
                (outer_hbm, outer),
                (wave_hbm, wave),
            )
        )
    ]
    for load in loads:
        load.start()

    def to_band(source, target, other, phase):
        return pltpu.make_async_remote_copy(
            src_ref=source,
            dst_ref=target,
            send_sem=send_sem.at[phase],
            recv_sem=recv_sem.at[phase],
            device_id=(other, my_lev),
            device_id_type=pl.DeviceIdType.MESH,
        )

    loads[0].wait()
    loads[1].wait()
    turned_column = column[...].astype(f32).T
    turned_weight = weight[...].T
    for h in range(2):
        request_out[pl.ds(h, band, stride=4), :] = turned_column[h * band : (h + 1) * band]
        request_out[pl.ds(2 + h, band, stride=4), :] = turned_weight[h * band : (h + 1) * band]
    mine = pltpu.make_async_copy(
        request_out.at[pl.ds(4 * me, 4)], request_in.at[pl.ds(4 * me, 4)], recv_sem.at[0]
    )
    mine.start()

    def send_request(i, carry):
        other = lax.rem(me + i, band)
        to_band(request_out.at[pl.ds(4 * other, 4)], request_in.at[pl.ds(4 * me, 4)], other, 0).start()
        return carry

    lax.fori_loop(1, band, send_request, 0)

    loads[2].wait()
    blocks = winds.shape[0] // 3
    for a in range(3):
        part = winds[pl.ds(a * blocks, blocks), :]
        table[:, a, :] = part
        table[:, 4 + a, :] = part
    loads[3].wait()
    pltpu.make_async_copy(request_in, request_in, recv_sem.at[0]).wait()

    sub = lax.broadcasted_iota(jnp.int32, (8, LANES), 0)
    lane = lax.broadcasted_iota(jnp.int32, (8, LANES), 1)
    upper = sub < 4
    own_group = (lane >> 5) == (sub & 3)

    def weigh(other):
        rows = [jnp.broadcast_to(request_in[pl.ds(4 * other + k, 1), :], (8, LANES)) for k in range(4)]
        where = jnp.where(upper, rows[0], rows[1]).astype(jnp.int32)
        scale = jnp.where(upper, rows[2], rows[3])
        within, block = where & (BLK - 1), where >> 7
        total = jnp.zeros((8, LANES), f32)
        for c in range(PER):
            piece = table[pick[other, pick_at + c]]
            total = jnp.where(block == c, take(piece, within), total)
        total = total * scale
        total = total + pltpu.roll(total, 64, 1)
        total = total + pltpu.roll(total, 32, 1)
        total = jnp.where(own_group, total, 0.0)
        total = total + pltpu.roll(total, 1, 0)
        total = total + pltpu.roll(total, 2, 0)
        reply_out[pl.ds(2 * other, 1), :] = total[3:4]
        reply_out[pl.ds(2 * other + 1, 1), :] = total[7:8]

    weigh(me)
    mine = pltpu.make_async_copy(
        reply_out.at[pl.ds(2 * me, 2)], reply_in.at[pl.ds(2 * me, 2)], recv_sem.at[1]
    )
    mine.start()
    group = 7

    def send_reply(i, carry):
        for u in range(group):
            weigh(lax.rem(me + 1 + i * group + u, band))
        for u in range(group):
            other = lax.rem(me + 1 + i * group + u, band)
            to_band(reply_out.at[pl.ds(2 * other, 2)], reply_in.at[pl.ds(2 * me, 2)], other, 1).start()
        return carry

    lax.fori_loop(0, (band - 1) // group, send_reply, 0)
    for load in loads[4:]:
        load.wait()
    pltpu.make_async_copy(reply_in, reply_in, recv_sem.at[1]).wait()

    number = cycle_ref[0]
    odd = (jnp.full((2 * band, LANES), number, jnp.int32) & 1) == 1
    odd_thin = (jnp.full((2 * M // LANES, 4 * band), number, jnp.int32) & 1) == 1

    def by_parity(table, *at):
        return jnp.where(odd, table[(0, *at)], table[(1, *at)])

    cos_theta = 4.0 / 3.0 - 2.0 * jnp.full((2 * band, LANES), number, jnp.int32).astype(f32) / (3.0 * NSIDE)
    sin_theta = jnp.sqrt(1.0 - cos_theta * cos_theta)
    component = lax.broadcasted_iota(jnp.int32, (2 * band, LANES), 1) >> 5
    samples = reply_in[...]
    east = samples * by_parity(coef, 0)
    north = samples * jnp.where(component == 2, sin_theta, -cos_theta * by_parity(coef, 1))
    high, low = high_low(jnp.concatenate([east, north], 0))
    section = dot(high, inner[0]) + dot(low, inner[0]) + dot(high, inner[1])
    cos, sin = by_parity(twiddle, 0), by_parity(twiddle, 1)
    cos, sin = jnp.concatenate([cos, cos], 0), jnp.concatenate([sin, sin], 0)
    real, imag = section[:, :LANES], section[:, LANES:]
    real, imag = real * cos + imag * sin, imag * cos - real * sin
    n = 2 * band
    high, low = high_low(
        jnp.concatenate(
            [jnp.concatenate([real[:n], real[n:]], 1), jnp.concatenate([imag[:n], imag[n:]], 1)], 0
        )
    )
    outer_hi = jnp.where(odd_thin, outer[0, 0], outer[0, 1])
    outer_lo = jnp.where(odd_thin, outer[1, 0], outer[1, 1])
    full = dot(outer_hi, high) + dot(outer_hi, low) + dot(outer_lo, high)
    full = full.astype(bf16).astype(f32)
    rows = M // LANES
    for f, (r, c) in enumerate(((0, 0), (1, 0), (0, 1), (1, 1))):
        spectrum[pl.ds(f * rows, rows), :] = full[r * rows : (r + 1) * rows, c * LANES : (c + 1) * LANES]

    wave_row, wave_lane = wave[...] >> 7, wave[...] & (LANES - 1)
    field = (lane >> 3) & 3
    spot = (lane >> 5) * 8 + (lane & 7)
    for h in range(rows // 8):
        row_of, lane_of = wave_row[8 * h : 8 * h + 8], wave_lane[8 * h : 8 * h + 8]
        ordered = []
        for f in range(4):
            picked = jnp.zeros((8, LANES), f32)
            for r in range(rows):
                source = jnp.broadcast_to(spectrum[pl.ds(f * rows + r, 1), :], (8, LANES))
                picked = jnp.where(row_of == r, take(source, lane_of), picked)
            ordered.append(picked)
        for b in range(4):
            packed = jnp.zeros((8, LANES), f32)
            for f in range(4):
                packed = jnp.where(field == f, take(ordered[f], spot + 32 * b), packed)
            rows_out[pl.ds(b * rows + 8 * h, 8), :] = packed

    def row_for(other):
        return lax.rem(other, 4) * rows + other // 4

    mine = pltpu.make_async_copy(rows_out.at[pl.ds(row_for(me), 1)], rows_in.at[pl.ds(me, 1)], recv_sem.at[2])
    mine.start()

    def send_rows(i, carry):
        other = lax.rem(me + i, band)
        to_band(rows_out.at[pl.ds(row_for(other), 1)], rows_in.at[pl.ds(me, 1)], other, 2).start()
        return carry

    lax.fori_loop(1, band, send_rows, 0)
    pltpu.make_async_copy(rows_in, rows_in, recv_sem.at[2]).wait()

    arrived = rows_in[...]
    turned[...] = jnp.concatenate([arrived, arrived], 0).T.reshape(turned.shape)
    mine = pltpu.make_async_copy(turned.at[my_lev], levels_in.at[:, my_lev], recv_sem.at[3])
    mine.start()

    def to_level(other):
        return pltpu.make_async_remote_copy(
            src_ref=turned.at[other],
            dst_ref=levels_in.at[:, my_lev],
            send_sem=send_sem.at[3],
            recv_sem=recv_sem.at[3],
            device_id=(me, other),
            device_id_type=pl.DeviceIdType.MESH,
        )

    for i in range(1, lev):
        to_level(lax.rem(my_lev + i, lev)).start()
    pltpu.make_async_copy(levels_in, levels_in, recv_sem.at[3]).wait()

    first = lax.broadcasted_iota(jnp.int32, (8, LANES), 1) < band
    sign_a, sign_b = (-1.0, 1.0, -1.0, 1.0), (-1.0, -1.0, 1.0, 1.0)
    for o in range(4):
        for v in range(lev):
            out_ref[pl.ds((o * lev + v) * 8, 8), :] = jnp.where(
                first, sign_a[o] * levels_in[o ^ 1, v], sign_b[o] * levels_in[o ^ 2, v]
            )

    pltpu.make_async_copy(request_out.at[pl.ds(0, 4 * (band - 1))], request_out.at[pl.ds(0, 4 * (band - 1))], send_sem.at[0]).wait()
    pltpu.make_async_copy(reply_out.at[pl.ds(0, 2 * (band - 1))], reply_out.at[pl.ds(0, 2 * (band - 1))], send_sem.at[1]).wait()
    pltpu.make_async_copy(rows_out.at[pl.ds(0, band - 1)], rows_out.at[pl.ds(0, band - 1)], send_sem.at[2]).wait()
    pltpu.make_async_copy(turned.at[pl.ds(0, lev - 1)], turned.at[pl.ds(0, lev - 1)], send_sem.at[3]).wait()


def legendre_kernel(owned, wave_ref, left_ref, a_ref, b_ref, div_ref, vort_ref):
    me = lax.axis_index("band") * lax.axis_size("lev") + lax.axis_index("lev")
    width = a_ref.shape[2]
    rows = left_ref.shape[0]
    left = left_ref[...]
    slot = lax.broadcasted_iota(jnp.int32, left.shape, 0) % owned
    pieces = [jnp.where(slot == i, left, 0.0).astype(bf16) for i in range(owned)]
    total = jnp.zeros((rows, width), f32)
    for i in range(0, owned, 2):
        right = jnp.concatenate([a_ref[i], b_ref[i], a_ref[i + 1], b_ref[i + 1]], 0)
        total = total + dot(jnp.concatenate([pieces[i], pieces[i + 1]], 1), right)
    lowest = jnp.zeros((owned, width), jnp.int32)
    row = lax.broadcasted_iota(jnp.int32, lowest.shape, 0)
    for i in range(owned):
        lowest = jnp.where(row == i, wave_ref[me * owned + i], lowest)
    degree = pl.program_id(0) * width + lax.broadcasted_iota(jnp.int32, lowest.shape, 1)
    keep = degree >= lowest
    half = rows // 2
    for r in range(0, half, owned):
        div_ref[r : r + owned] = jnp.where(keep, total[r : r + owned], 0.0)
        vort_ref[r : r + owned] = jnp.where(keep, total[half + r : half + r + owned], 0.0)


def local(winds, remap_w, remap_col, block_pick, cycle_ids, wave_ids, legendre_a, legendre_b):
    band, lev = lax.axis_size("band"), lax.axis_size("lev")
    coef, twiddle, inner, outer = tables(band)
    columns = winds.shape[2]
    owned, cycles, degrees = legendre_a.shape
    blocks = columns // BLK
    hbm = pl.BlockSpec(memory_space=pltpu.HBM)
    smem = pl.BlockSpec(memory_space=pltpu.SMEM)
    vmem = pl.BlockSpec(memory_space=pltpu.VMEM)
    left = pl.pallas_call(
        functools.partial(modes_kernel, band, lev),
        out_shape=jax.ShapeDtypeStruct((4 * lev * owned, 2 * cycles), f32),
        in_specs=[smem] + [hbm] * 9,
        out_specs=vmem,
        scratch_shapes=[
            pltpu.VMEM((3 * blocks, BLK), f32),
            pltpu.VMEM((2 * band, LANES), f32),
            pltpu.VMEM((2 * band, LANES), jnp.int32),
            pltpu.SMEM((band, 2 * LANES), jnp.int32),
            pltpu.VMEM((M // LANES, LANES), jnp.int32),
            pltpu.VMEM(coef.shape, f32),
            pltpu.VMEM(twiddle.shape, f32),
            pltpu.VMEM(inner.shape, bf16),
            pltpu.VMEM(outer.shape, bf16),
            pltpu.VMEM((blocks, 8, BLK), f32),
            pltpu.VMEM((4 * band, LANES), f32),
            pltpu.VMEM((4 * band, LANES), f32),
            pltpu.VMEM((2 * band, LANES), f32),
            pltpu.VMEM((2 * band, LANES), f32),
            pltpu.VMEM((4 * M // LANES, LANES), f32),
            pltpu.VMEM((band, LANES), f32),
            pltpu.VMEM((band, LANES), f32),
            pltpu.VMEM((lev, 4, owned, LANES), f32),
            pltpu.VMEM((4, lev, owned, LANES), f32),
            pltpu.SemaphoreType.DMA((9,)),
            pltpu.SemaphoreType.DMA((4,)),
            pltpu.SemaphoreType.DMA((4,)),
        ],
        compiler_params=pltpu.CompilerParams(has_side_effects=True, vmem_limit_bytes=60 * 2**20),
        name="modes",
    )(
        cycle_ids,
        winds.reshape(3 * blocks, BLK),
        remap_w.reshape(2 * band, LANES),
        remap_col.reshape(2 * band, LANES),
        block_pick,
        wave_ids.reshape(M // LANES, LANES),
        coef,
        twiddle,
        inner,
        outer,
    )
    width = 512
    shape = jax.ShapeDtypeStruct((2 * lev * owned, degrees), f32)
    divergence, vorticity = pl.pallas_call(
        functools.partial(legendre_kernel, owned),
        grid=(degrees // width,),
        out_shape=(shape, shape),
        in_specs=[
            smem,
            pl.BlockSpec((4 * lev * owned, 2 * cycles), lambda j: (0, 0)),
            pl.BlockSpec((owned, cycles, width), lambda j: (0, 0, j)),
            pl.BlockSpec((owned, cycles, width), lambda j: (0, 0, j)),
        ],
        out_specs=(
            pl.BlockSpec((2 * lev * owned, width), lambda j: (0, j)),
            pl.BlockSpec((2 * lev * owned, width), lambda j: (0, j)),
        ),
        compiler_params=pltpu.CompilerParams(vmem_limit_bytes=60 * 2**20),
        name="legendre",
    )(wave_ids, left, legendre_a, legendre_b)
    whole = (2, lev, owned, degrees)
    return divergence.reshape(whole), vorticity.reshape(whole)


def solution(mesh):
    placed = (
        P(None, "lev", "band"),
        P(None, "band", None),
        P(None, "band", None),
        P(),
        P("band"),
        P(),
        P(("band", "lev"), None, None),
        P(("band", "lev"), None, None),
    )
    return jax.shard_map(
        local,
        mesh=mesh,
        in_specs=placed,
        out_specs=(P(None, None, ("band", "lev"), None), P(None, None, ("band", "lev"), None)),
        check_vma=False,
    )
```

time: 229 us -> 54.2 us (0.24)
  local copies, waits for them, and re-layouts: 122 us -> 0 us
  waiting for transfers between devices: 57.6 us -> 0 us
  Pallas kernels: 0 us -> 52.8 us
  starting transfers between devices: 23.8 us -> 0 us
  other arithmetic: 16.7 us -> 0 us
  matrix products: 5.48 us -> 0 us
    gather x4 -> x0, local copies, waits for them, and re-layouts: 77.2 us -> none  [the longest x1 69.8 us: local(): jnp.take(flattened, tap_index.reshape(-1), axis=2)]
    all_to_all x3 -> x0, waiting for transfers between devices: 57.6 us -> none  [the longest x1 27.9 us: local(): lax.all_to_all(outgoing_modes, 'band', split_axis=3, concat_axis=2, tiled...]
    pallas_call x0 -> x2, Pallas kernels: none -> 52.8 us  [the longest x1 48.3 us: local(): pl.pallas_call(functools.partial(modes_kernel, band, lev), out_shape=jax....]
    all_to_all x5 -> x0, local copies, waits for them, and re-layouts: 24.6 us -> none  [the longest x1 23.8 us: local(): lax.all_to_all(outgoing, 'band', split_axis=2, concat_axis=2, tiled=True)]
    all_to_all x3 -> x0, starting transfers between devices: 23.8 us -> none  [the longest x1 13.2 us: local(): lax.all_to_all(outgoing, 'band', split_axis=2, concat_axis=2, tiled=True)]
    slice x6 -> x0, local copies, waits for them, and re-layouts: 8.4 us -> none  [the longest x2 8.1 us: local(): vort_real = jnp.where(upper, -part_a[:, :, 3] + part_b[:, :, 0], 0.0)]
    reduce_sum x1 -> x0, other arithmetic: 6.93 us -> none  [local(): cartesian_flat = jnp.sum(sampled * weights[None, None], axis=2)]
    reshape x5 -> x0, local copies, waits for them, and re-layouts: 6.11 us -> none  [the longest x1 2.03 us: select_waves(): return picked.reshape(lead + (order.shape[0],))]
  transfers between devices with their start and end apart: 3 -> 0, of which waited for: 3 -> 0; matrix products, arithmetic and copies ran while one was open for 2% -> 0% of each run, Pallas kernels for 0% -> 0%
where the time goes in v1:
time: 54.2 us; the launch traced here: 54.1 us
  Pallas kernels  52.8 us (97%)
  between operations  1.29 us (2%)
    pallas_call x1, Pallas kernels, local(): pl.pallas_call(functools.partial(modes_kernel, band, lev), out_shape=jax....  48.3 us
    pallas_call x1, Pallas kernels, local(): pl.pallas_call(functools.partial(legendre_kernel, owned), grid=(degrees /...  4.51 us

profile of v1, /device:TPU:1, one launch (start us, length us, event | category | flops | bytes accessed | tf_op | source)
XLA Modules:
  0.0 54.1 jit_solution(1980874345684436701)
XLA Ops:
  1.3 48.3 %modes.1.left_ref = f32[128,128]{1,0:T(8,128)} custom-call(s32[1]{0:T(128)S(6)} %copy.14.cycle_ref, f32[768,128]{1,0:T(8,128)} %bitcast.6, f32[128,128]{1,0:T(8,128)} %bitcast.7, s32[128,128]{1,0:T(8,128)} %bitcast.8, s32[64,768]{1,0:T(8,128)} %pick_hbm.1, s32[16,128]{1,0:T(8,128)} %bitcast.9, f32[2,2,128,128]{3,2,1,0:T(8,128)} %constant.8.clone.coef_hbm, ...), custom_call_target="tpu_custom_call" | custom-call | tf_op jit(solution)/shard_map/modes/pallas_call | solution.py:350
  49.6 4.5 %legendre.1 = (f32[64,2048]{1,0:T(8,128)}, f32[64,2048]{1,0:T(8,128)}) custom-call(s32[2048]{0:T(1024)} %wave_ref.1, f32[128,128]{1,0:T(8,128)} %modes.1.left_ref, bf16[8,64,2048]{2,1,0:T(8,128)(2,1)} %a_ref.1, bf16[8,64,2048]{2,1,0:T(8,128)(2,1)} %b_ref.1), custom_call_target="tpu_custom_call" | custom-call | tf_op jit(solution)/shard_map/legendre/pallas_call | solution.py:395

commit v2 on v1

--- a/solution.py
+++ b/solution.py
@@ -115,6 +115,18 @@
 ):
     me = lax.axis_index("band")
     my_lev = lax.axis_index("lev")
+    barrier = pltpu.get_barrier_semaphore()
+
+    def greet(i, carry):
+        other = lax.rem(me + i, band)
+        pl.semaphore_signal(barrier, 1, device_id=(other, my_lev), device_id_type=pl.DeviceIdType.MESH)
+        return carry
+
+    lax.fori_loop(1, band, greet, 0)
+    for i in range(1, lev):
+        other = lax.rem(my_lev + i, lev)
+        pl.semaphore_signal(barrier, 1, device_id=(me, other), device_id_type=pl.DeviceIdType.MESH)
+
     window = jnp.minimum(me * PER // LANES, PER * band // LANES - 2)
     pick_at = me * PER - window * LANES
     loads = [
@@ -153,24 +165,24 @@
     for h in range(2):
         request_out[pl.ds(h, band, stride=4), :] = turned_column[h * band : (h + 1) * band]
         request_out[pl.ds(2 + h, band, stride=4), :] = turned_weight[h * band : (h + 1) * band]
-    mine = pltpu.make_async_copy(
-        request_out.at[pl.ds(4 * me, 4)], request_in.at[pl.ds(4 * me, 4)], recv_sem.at[0]
-    )
-    mine.start()
-
-    def send_request(i, carry):
-        other = lax.rem(me + i, band)
-        to_band(request_out.at[pl.ds(4 * other, 4)], request_in.at[pl.ds(4 * me, 4)], other, 0).start()
-        return carry
-
-    lax.fori_loop(1, band, send_request, 0)
-
     loads[2].wait()
     blocks = winds.shape[0] // 3
     for a in range(3):
         part = winds[pl.ds(a * blocks, blocks), :]
         table[:, a, :] = part
         table[:, 4 + a, :] = part
+    pl.semaphore_wait(barrier, band - 1 + lev - 1)
+    mine = pltpu.make_async_copy(
+        request_out.at[pl.ds(4 * me, 4)], request_in.at[pl.ds(4 * me, 4)], recv_sem.at[0]
+    )
+    mine.start()
+
+    def send_request(i, carry):
+        other = lax.rem(me + i, band)
+        to_band(request_out.at[pl.ds(4 * other, 4)], request_in.at[pl.ds(4 * me, 4)], other, 0).start()
+        return carry
+
+    lax.fori_loop(1, band, send_request, 0)
     loads[3].wait()
     pltpu.make_async_copy(request_in, request_in, recv_sem.at[0]).wait()
 
@@ -376,7 +388,7 @@
             pltpu.SemaphoreType.DMA((4,)),
             pltpu.SemaphoreType.DMA((4,)),
         ],
-        compiler_params=pltpu.CompilerParams(has_side_effects=True, vmem_limit_bytes=60 * 2**20),
+        compiler_params=pltpu.CompilerParams(collective_id=0, has_side_effects=True, vmem_limit_bytes=60 * 2**20),
         name="modes",
     )(
         cycle_ids,

time: 54.2 us -> 44.9 us (0.83)
  Pallas kernels: 52.8 us -> 43.4 us
    pallas_call x1, Pallas kernels: 48.3 us -> 38.9 us  [local(): pl.pallas_call(functools.partial(modes_kernel, band, lev), out_shape=jax....]
where the time goes in v2:
time: 44.9 us; the launch traced here: 44.7 us
  Pallas kernels  43.4 us (97%)
  between operations  1.29 us (3%)
    pallas_call x1, Pallas kernels, local(): pl.pallas_call(functools.partial(modes_kernel, band, lev), out_shape=jax....  38.9 us
    pallas_call x1, Pallas kernels, local(): pl.pallas_call(functools.partial(legendre_kernel, owned), grid=(degrees /...  4.5 us

profile of v2, /device:TPU:1, one launch (start us, length us, event | category | flops | bytes accessed | tf_op | source)
XLA Modules:
  0.0 44.7 jit_solution(8517211785557687554)
XLA Ops:
  1.3 38.9 %modes.1.left_ref = f32[128,128]{1,0:T(8,128)} custom-call(s32[1]{0:T(128)S(6)} %copy.14.cycle_ref, f32[768,128]{1,0:T(8,128)} %bitcast.6, f32[128,128]{1,0:T(8,128)} %bitcast.7, s32[128,128]{1,0:T(8,128)} %bitcast.8, s32[64,768]{1,0:T(8,128)} %pick_hbm.1, s32[16,128]{1,0:T(8,128)} %bitcast.9, f32[2,2,128,128]{3,2,1,0:T(8,128)} %constant.8.clone.coef_hbm, ...), custom_call_target="tpu_custom_call" | custom-call | tf_op jit(solution)/shard_map/modes/pallas_call | solution.py:362
  40.2 4.5 %legendre.1 = (f32[64,2048]{1,0:T(8,128)}, f32[64,2048]{1,0:T(8,128)}) custom-call(s32[2048]{0:T(1024)} %wave_ref.1, f32[128,128]{1,0:T(8,128)} %modes.1.left_ref, bf16[8,64,2048]{2,1,0:T(8,128)(2,1)} %a_ref.1, bf16[8,64,2048]{2,1,0:T(8,128)(2,1)} %b_ref.1), custom_call_target="tpu_custom_call" | custom-call | tf_op jit(solution)/shard_map/legendre/pallas_call | solution.py:407

commit v3 on v2

--- a/solution.py
+++ b/solution.py
@@ -16,6 +16,7 @@
 PER = 12
 TAPS = 4
 LANES = 128
+WIDTH = 512
 
 f32 = jnp.float32
 bf16 = jnp.bfloat16
@@ -89,7 +90,11 @@
     twiddle_hbm,
     inner_hbm,
     outer_hbm,
+    a_hbm,
+    b_hbm,
     out_ref,
+    leg_a,
+    leg_b,
     winds,
     weight,
     column,
@@ -112,6 +117,7 @@
     local_sem,
     send_sem,
     recv_sem,
+    legendre_sem,
 ):
     me = lax.axis_index("band")
     my_lev = lax.axis_index("lev")
@@ -183,6 +189,12 @@
         return carry
 
     lax.fori_loop(1, band, send_request, 0)
+    legendre_loads = [
+        pltpu.make_async_copy(a_hbm, leg_a, legendre_sem.at[0]),
+        pltpu.make_async_copy(b_hbm, leg_b, legendre_sem.at[1]),
+    ]
+    for load in legendre_loads:
+        load.start()
     loads[3].wait()
     pltpu.make_async_copy(request_in, request_in, recv_sem.at[0]).wait()
 
@@ -321,33 +333,42 @@
                 first, sign_a[o] * levels_in[o ^ 1, v], sign_b[o] * levels_in[o ^ 2, v]
             )
 
+    for load in legendre_loads:
+        load.wait()
     pltpu.make_async_copy(request_out.at[pl.ds(0, 4 * (band - 1))], request_out.at[pl.ds(0, 4 * (band - 1))], send_sem.at[0]).wait()
     pltpu.make_async_copy(reply_out.at[pl.ds(0, 2 * (band - 1))], reply_out.at[pl.ds(0, 2 * (band - 1))], send_sem.at[1]).wait()
     pltpu.make_async_copy(rows_out.at[pl.ds(0, band - 1)], rows_out.at[pl.ds(0, band - 1)], send_sem.at[2]).wait()
     pltpu.make_async_copy(turned.at[pl.ds(0, lev - 1)], turned.at[pl.ds(0, lev - 1)], send_sem.at[3]).wait()
 
 
-def legendre_kernel(owned, wave_ref, left_ref, a_ref, b_ref, div_ref, vort_ref):
+def legendre_kernel(wave_ref, left_ref, a_ref, b_ref, div_hbm, vort_hbm, div, vort, store_sem):
     me = lax.axis_index("band") * lax.axis_size("lev") + lax.axis_index("lev")
-    width = a_ref.shape[2]
-    rows = left_ref.shape[0]
+    owned, _, degrees = a_ref.shape
+    half = left_ref.shape[0] // 2
     left = left_ref[...]
     slot = lax.broadcasted_iota(jnp.int32, left.shape, 0) % owned
     pieces = [jnp.where(slot == i, left, 0.0).astype(bf16) for i in range(owned)]
-    total = jnp.zeros((rows, width), f32)
-    for i in range(0, owned, 2):
-        right = jnp.concatenate([a_ref[i], b_ref[i], a_ref[i + 1], b_ref[i + 1]], 0)
-        total = total + dot(jnp.concatenate([pieces[i], pieces[i + 1]], 1), right)
-    lowest = jnp.zeros((owned, width), jnp.int32)
-    row = lax.broadcasted_iota(jnp.int32, lowest.shape, 0)
+    pieces = [jnp.concatenate(pieces[i : i + 2], 1) for i in range(0, owned, 2)]
+    row = lax.broadcasted_iota(jnp.int32, (owned, WIDTH), 0)
+    lowest = jnp.zeros((owned, WIDTH), jnp.int32)
     for i in range(owned):
         lowest = jnp.where(row == i, wave_ref[me * owned + i], lowest)
-    degree = pl.program_id(0) * width + lax.broadcasted_iota(jnp.int32, lowest.shape, 1)
-    keep = degree >= lowest
-    half = rows // 2
-    for r in range(0, half, owned):
-        div_ref[r : r + owned] = jnp.where(keep, total[r : r + owned], 0.0)
-        vort_ref[r : r + owned] = jnp.where(keep, total[half + r : half + r + owned], 0.0)
+    stores = []
+    for j in range(degrees // WIDTH):
+        at = pl.ds(j * WIDTH, WIDTH)
+        total = jnp.zeros((2 * half, WIDTH), f32)
+        for i in range(0, owned, 2):
+            right = jnp.concatenate([a_ref[i, :, at], b_ref[i, :, at], a_ref[i + 1, :, at], b_ref[i + 1, :, at]], 0)
+            total = total + dot(pieces[i // 2], right)
+        keep = j * WIDTH + lax.broadcasted_iota(jnp.int32, (owned, WIDTH), 1) >= lowest
+        for r in range(0, half, owned):
+            div[r : r + owned, at] = jnp.where(keep, total[r : r + owned], 0.0)
+            vort[r : r + owned, at] = jnp.where(keep, total[half + r : half + r + owned], 0.0)
+        for k, (source, target) in enumerate(((div, div_hbm), (vort, vort_hbm))):
+            stores.append(pltpu.make_async_copy(source.at[:, at], target.at[:, at], store_sem.at[2 * j + k]))
+            stores[-1].start()
+    for store in stores:
+        store.wait()
 
 
 def local(winds, remap_w, remap_col, block_pick, cycle_ids, wave_ids, legendre_a, legendre_b):
@@ -359,11 +380,15 @@
     hbm = pl.BlockSpec(memory_space=pltpu.HBM)
     smem = pl.BlockSpec(memory_space=pltpu.SMEM)
     vmem = pl.BlockSpec(memory_space=pltpu.VMEM)
-    left = pl.pallas_call(
+    left, leg_a, leg_b = pl.pallas_call(
         functools.partial(modes_kernel, band, lev),
-        out_shape=jax.ShapeDtypeStruct((4 * lev * owned, 2 * cycles), f32),
-        in_specs=[smem] + [hbm] * 9,
-        out_specs=vmem,
+        out_shape=(
+            pltpu.VMEM((4 * lev * owned, 2 * cycles), f32),
+            pltpu.VMEM(legendre_a.shape, bf16),
+            pltpu.VMEM(legendre_b.shape, bf16),
+        ),
+        in_specs=[smem] + [hbm] * 11,
+        out_specs=(vmem, vmem, vmem),
         scratch_shapes=[
             pltpu.VMEM((3 * blocks, BLK), f32),
             pltpu.VMEM((2 * band, LANES), f32),
@@ -387,8 +412,9 @@
             pltpu.SemaphoreType.DMA((9,)),
             pltpu.SemaphoreType.DMA((4,)),
             pltpu.SemaphoreType.DMA((4,)),
+            pltpu.SemaphoreType.DMA((2,)),
         ],
-        compiler_params=pltpu.CompilerParams(collective_id=0, has_side_effects=True, vmem_limit_bytes=60 * 2**20),
+        compiler_params=pltpu.CompilerParams(collective_id=0, has_side_effects=True, vmem_limit_bytes=52 * 2**20),
         name="modes",
     )(
         cycle_ids,
@@ -401,26 +427,23 @@
         twiddle,
         inner,
         outer,
-    )
-    width = 512
+        legendre_a,
+        legendre_b,
+    )
     shape = jax.ShapeDtypeStruct((2 * lev * owned, degrees), f32)
     divergence, vorticity = pl.pallas_call(
-        functools.partial(legendre_kernel, owned),
-        grid=(degrees // width,),
+        legendre_kernel,
         out_shape=(shape, shape),
-        in_specs=[
-            smem,
-            pl.BlockSpec((4 * lev * owned, 2 * cycles), lambda j: (0, 0)),
-            pl.BlockSpec((owned, cycles, width), lambda j: (0, 0, j)),
-            pl.BlockSpec((owned, cycles, width), lambda j: (0, 0, j)),
+        in_specs=[smem, vmem, vmem, vmem],
+        out_specs=(hbm, hbm),
+        scratch_shapes=[
+            pltpu.VMEM(shape.shape, f32),
+            pltpu.VMEM(shape.shape, f32),
+            pltpu.SemaphoreType.DMA((2 * degrees // WIDTH,)),
         ],
-        out_specs=(
-            pl.BlockSpec((2 * lev * owned, width), lambda j: (0, j)),
-            pl.BlockSpec((2 * lev * owned, width), lambda j: (0, j)),
-        ),
-        compiler_params=pltpu.CompilerParams(vmem_limit_bytes=60 * 2**20),
+        compiler_params=pltpu.CompilerParams(vmem_limit_bytes=32 * 2**20),
         name="legendre",
-    )(wave_ids, left, legendre_a, legendre_b)
+    )(wave_ids, left, leg_a, leg_b)
     whole = (2, lev, owned, degrees)
     return divergence.reshape(whole), vorticity.reshape(whole)
 

time: 44.9 us -> 41.9 us (0.933)
  Pallas kernels: 43.4 us -> 40.5 us
    pallas_call x2, Pallas kernels: 43.4 us -> 40.5 us  [the longest x1 38.3 us: local(): pl.pallas_call(functools.partial(modes_kernel, band, lev), out_shape=(plt...]
where the time goes in v3:
time: 41.9 us; the launch traced here: 41.8 us
  Pallas kernels  40.5 us (97%)
  between operations  1.3 us (3%)
    pallas_call x1, Pallas kernels, local(): pl.pallas_call(functools.partial(modes_kernel, band, lev), out_shape=(plt...  38.3 us
    pallas_call x1, Pallas kernels, local(): pl.pallas_call(legendre_kernel, out_shape=(shape, shape), in_specs=[smem,...  2.15 us

profile of v3, /device:TPU:1, one launch (start us, length us, event | category | flops | bytes accessed | tf_op | source)
XLA Modules:
  0.0 41.8 jit_solution(4557525620247588987)
XLA Ops:
  1.3 0.0 copy-start
  1.3 38.3 %modes.1 = (f32[128,128]{1,0:T(8,128)S(1)}, bf16[8,64,2048]{2,1,0:T(8,128)(2,1)S(1)}, bf16[8,64,2048]{2,1,0:T(8,128)(2,1)S(1)}) custom-call(s32[1]{0:T(128)S(6)} %copy.14.cycle_ref, f32[768,128]{1,0:T(8,128)} %bitcast.7, f32[128,128]{1,0:T(8,128)} %bitcast.8, s32[128,128]{1,0:T(8,128)} %bitcast.9, s32[64,768]{1,0:T(8,128)} %pick_hbm.1, s32[16,128]{1,0:T(8,128)} %bitcast.6, ...), custom_call_target="tpu_custom_call" | custom-call | tf_op jit(solution)/shard_map/modes/pallas_call | solution.py:383
  39.6 0.0 copy-done
  39.7 2.1 %legendre.1 = (f32[64,2048]{1,0:T(8,128)}, f32[64,2048]{1,0:T(8,128)}) custom-call(s32[2048]{0:T(1024)S(1)} %copy-done, f32[128,128]{1,0:T(8,128)S(1)} %get-tuple-element.7.left_ref, bf16[8,64,2048]{2,1,0:T(8,128)(2,1)S(1)} %get-tuple-element.8.a_ref, bf16[8,64,2048]{2,1,0:T(8,128)(2,1)S(1)} %get-tuple-element.9.b_ref), custom_call_target="tpu_custom_call" | custom-call | tf_op jit(solution)/shard_map/legendre/pallas_call | solution.py:434
Async XLA Ops:
  1.3 38.4 %copy-start = (s32[2048]{0:T(1024)S(1)}, s32[2048]{0:T(1024)}, u32[]{:S(2)}) copy-start(s32[2048]{0:T(1024)} %wave_ref.1) | copy-start | bytes 24580

commit v4 on v3

--- a/solution.py
+++ b/solution.py
@@ -16,6 +16,7 @@
 PER = 12
 TAPS = 4
 LANES = 128
+GROUP = 8
 WIDTH = 512
 
 f32 = jnp.float32
@@ -66,6 +67,10 @@
 
 def dot(a, b):
     return jnp.dot(a, b, preferred_element_type=f32)
+
+
+def far_first(i, count):
+    return count // 2 + (1 - 2 * (i % 2)) * ((i + 1) // 2)
 
 
 def high_low(x):
@@ -112,8 +117,6 @@
     spectrum,
     rows_out,
     rows_in,
-    turned,
-    levels_in,
     local_sem,
     send_sem,
     recv_sem,
@@ -123,12 +126,27 @@
     my_lev = lax.axis_index("lev")
     barrier = pltpu.get_barrier_semaphore()
 
-    def greet(i, carry):
-        other = lax.rem(me + i, band)
-        pl.semaphore_signal(barrier, 1, device_id=(other, my_lev), device_id_type=pl.DeviceIdType.MESH)
-        return carry
-
-    lax.fori_loop(1, band, greet, 0)
+    plane, place = lax.div(me, GROUP), lax.rem(me, GROUP)
+    planes = band // GROUP
+    places = [lax.rem(place + far_first(k, GROUP), GROUP) for k in range(GROUP)]
+    my_levels = [lax.rem(my_lev + far_first(k, lev), lev) for k in range(lev)]
+
+    def each_plane(act):
+        def step(k, carry):
+            odd = lax.rem(k, 2)
+            ahead = planes // 2 + (1 - 2 * odd) * lax.div(k + 1, 2)
+            base = lax.rem(plane + ahead, planes) * GROUP
+            act([base + p for p in places])
+            return carry
+
+        lax.fori_loop(0, planes - 1, step, 0)
+        act([plane * GROUP + p for p in places[:-1]])
+
+    def greet(others):
+        for other in others:
+            pl.semaphore_signal(barrier, 1, device_id=(other, my_lev), device_id_type=pl.DeviceIdType.MESH)
+
+    each_plane(greet)
     for i in range(1, lev):
         other = lax.rem(my_lev + i, lev)
         pl.semaphore_signal(barrier, 1, device_id=(me, other), device_id_type=pl.DeviceIdType.MESH)
@@ -183,12 +201,11 @@
     )
     mine.start()
 
-    def send_request(i, carry):
-        other = lax.rem(me + i, band)
-        to_band(request_out.at[pl.ds(4 * other, 4)], request_in.at[pl.ds(4 * me, 4)], other, 0).start()
-        return carry
-
-    lax.fori_loop(1, band, send_request, 0)
+    def send_request(others):
+        for other in others:
+            to_band(request_out.at[pl.ds(4 * other, 4)], request_in.at[pl.ds(4 * me, 4)], other, 0).start()
+
+    each_plane(send_request)
     legendre_loads = [
         pltpu.make_async_copy(a_hbm, leg_a, legendre_sem.at[0]),
         pltpu.make_async_copy(b_hbm, leg_b, legendre_sem.at[1]),
@@ -221,22 +238,18 @@
         reply_out[pl.ds(2 * other, 1), :] = total[3:4]
         reply_out[pl.ds(2 * other + 1, 1), :] = total[7:8]
 
+    def send_reply(others):
+        for other in others:
+            weigh(other)
+        for other in others:
+            to_band(reply_out.at[pl.ds(2 * other, 2)], reply_in.at[pl.ds(2 * me, 2)], other, 1).start()
+
+    each_plane(send_reply)
     weigh(me)
     mine = pltpu.make_async_copy(
         reply_out.at[pl.ds(2 * me, 2)], reply_in.at[pl.ds(2 * me, 2)], recv_sem.at[1]
     )
     mine.start()
-    group = 7
-
-    def send_reply(i, carry):
-        for u in range(group):
-            weigh(lax.rem(me + 1 + i * group + u, band))
-        for u in range(group):
-            other = lax.rem(me + 1 + i * group + u, band)
-            to_band(reply_out.at[pl.ds(2 * other, 2)], reply_in.at[pl.ds(2 * me, 2)], other, 1).start()
-        return carry
-
-    lax.fori_loop(0, (band - 1) // group, send_reply, 0)
     for load in loads[4:]:
         load.wait()
     pltpu.make_async_copy(reply_in, reply_in, recv_sem.at[1]).wait()
@@ -293,52 +306,54 @@
             rows_out[pl.ds(b * rows + 8 * h, 8), :] = packed
 
     def row_for(other):
-        return lax.rem(other, 4) * rows + other // 4
-
-    mine = pltpu.make_async_copy(rows_out.at[pl.ds(row_for(me), 1)], rows_in.at[pl.ds(me, 1)], recv_sem.at[2])
+        return lax.rem(other, 4) * rows + lax.div(other, 4)
+
+    def send_row(other, levels):
+        for v in levels:
+            pltpu.make_async_remote_copy(
+                src_ref=rows_out.at[pl.ds(row_for(other), 1)],
+                dst_ref=rows_in.at[pl.ds(my_lev * band + me, 1)],
+                send_sem=send_sem.at[2],
+                recv_sem=recv_sem.at[2],
+                device_id=(other, v),
+                device_id_type=pl.DeviceIdType.MESH,
+            ).start()
+
+    def send_rows(others):
+        for other in others:
+            send_row(other, my_levels)
+
+    each_plane(send_rows)
+    send_row(me, my_levels[:-1])
+    mine = pltpu.make_async_copy(
+        rows_out.at[pl.ds(row_for(me), 1)], rows_in.at[pl.ds(my_lev * band + me, 1)], recv_sem.at[2]
+    )
     mine.start()
-
-    def send_rows(i, carry):
-        other = lax.rem(me + i, band)
-        to_band(rows_out.at[pl.ds(row_for(other), 1)], rows_in.at[pl.ds(me, 1)], other, 2).start()
-        return carry
-
-    lax.fori_loop(1, band, send_rows, 0)
     pltpu.make_async_copy(rows_in, rows_in, recv_sem.at[2]).wait()
 
-    arrived = rows_in[...]
-    turned[...] = jnp.concatenate([arrived, arrived], 0).T.reshape(turned.shape)
-    mine = pltpu.make_async_copy(turned.at[my_lev], levels_in.at[:, my_lev], recv_sem.at[3])
-    mine.start()
-
-    def to_level(other):
-        return pltpu.make_async_remote_copy(
-            src_ref=turned.at[other],
-            dst_ref=levels_in.at[:, my_lev],
-            send_sem=send_sem.at[3],
-            recv_sem=recv_sem.at[3],
-            device_id=(me, other),
-            device_id_type=pl.DeviceIdType.MESH,
-        )
-
-    for i in range(1, lev):
-        to_level(lax.rem(my_lev + i, lev)).start()
-    pltpu.make_async_copy(levels_in, levels_in, recv_sem.at[3]).wait()
-
-    first = lax.broadcasted_iota(jnp.int32, (8, LANES), 1) < band
+    level = lax.broadcasted_iota(jnp.int32, (band, LANES), 1) >> 5
+    merged = jnp.zeros((band, LANES), f32)
+    for v in range(lev):
+        shifted = pltpu.roll(rows_in[pl.ds(v * band, band), :], lax.rem(v - my_lev + lev, lev) * 32, 1)
+        merged = jnp.where(level == v, shifted, merged)
+    turned = jnp.concatenate([merged, merged], 0).T
+    first = lane < band
     sign_a, sign_b = (-1.0, 1.0, -1.0, 1.0), (-1.0, -1.0, 1.0, 1.0)
+
+    def piece_of(v, f):
+        return turned[(v * 4 + f) * 8 : (v * 4 + f) * 8 + 8]
+
     for o in range(4):
         for v in range(lev):
             out_ref[pl.ds((o * lev + v) * 8, 8), :] = jnp.where(
-                first, sign_a[o] * levels_in[o ^ 1, v], sign_b[o] * levels_in[o ^ 2, v]
+                first, sign_a[o] * piece_of(v, o ^ 1), sign_b[o] * piece_of(v, o ^ 2)
             )
-
     for load in legendre_loads:
         load.wait()
     pltpu.make_async_copy(request_out.at[pl.ds(0, 4 * (band - 1))], request_out.at[pl.ds(0, 4 * (band - 1))], send_sem.at[0]).wait()
     pltpu.make_async_copy(reply_out.at[pl.ds(0, 2 * (band - 1))], reply_out.at[pl.ds(0, 2 * (band - 1))], send_sem.at[1]).wait()
-    pltpu.make_async_copy(rows_out.at[pl.ds(0, band - 1)], rows_out.at[pl.ds(0, band - 1)], send_sem.at[2]).wait()
-    pltpu.make_async_copy(turned.at[pl.ds(0, lev - 1)], turned.at[pl.ds(0, lev - 1)], send_sem.at[3]).wait()
+    sent = rows_in.at[pl.ds(0, lev * band - 1)]
+    pltpu.make_async_copy(sent, sent, send_sem.at[2]).wait()
 
 
 def legendre_kernel(wave_ref, left_ref, a_ref, b_ref, div_hbm, vort_hbm, div, vort, store_sem):
@@ -406,12 +421,10 @@
             pltpu.VMEM((2 * band, LANES), f32),
             pltpu.VMEM((4 * M // LANES, LANES), f32),
             pltpu.VMEM((band, LANES), f32),
-            pltpu.VMEM((band, LANES), f32),
-            pltpu.VMEM((lev, 4, owned, LANES), f32),
-            pltpu.VMEM((4, lev, owned, LANES), f32),
+            pltpu.VMEM((lev * band, LANES), f32),
             pltpu.SemaphoreType.DMA((9,)),
-            pltpu.SemaphoreType.DMA((4,)),
-            pltpu.SemaphoreType.DMA((4,)),
+            pltpu.SemaphoreType.DMA((3,)),
+            pltpu.SemaphoreType.DMA((3,)),
             pltpu.SemaphoreType.DMA((2,)),
         ],
         compiler_params=pltpu.CompilerParams(collective_id=0, has_side_effects=True, vmem_limit_bytes=52 * 2**20),

time: 41.9 us -> 38.4 us (0.916)
  Pallas kernels: 40.5 us -> 37 us
    pallas_call x1, Pallas kernels: 38.3 us -> 34.9 us  [local(): pl.pallas_call(functools.partial(modes_kernel, band, lev), out_shape=(plt...]
where the time goes in v4:
time: 38.4 us; the launch traced here: 38.3 us
  Pallas kernels  37 us (96%)
  between operations  1.3 us (3%)
    pallas_call x1, Pallas kernels, local(): pl.pallas_call(functools.partial(modes_kernel, band, lev), out_shape=(plt...  34.9 us
    pallas_call x1, Pallas kernels, local(): pl.pallas_call(legendre_kernel, out_shape=(shape, shape), in_specs=[smem,...  2.15 us

profile of v4, /device:TPU:1, one launch (start us, length us, event | category | flops | bytes accessed | tf_op | source)
XLA Modules:
  0.0 38.3 jit_solution(11160828827428857960)
XLA Ops:
  1.3 0.0 copy-start
  1.3 34.9 %modes.1 = (f32[128,128]{1,0:T(8,128)S(1)}, bf16[8,64,2048]{2,1,0:T(8,128)(2,1)S(1)}, bf16[8,64,2048]{2,1,0:T(8,128)(2,1)S(1)}) custom-call(s32[1]{0:T(128)S(6)} %copy.14.cycle_ref, f32[768,128]{1,0:T(8,128)} %bitcast.7, f32[128,128]{1,0:T(8,128)} %bitcast.8, s32[128,128]{1,0:T(8,128)} %bitcast.9, s32[64,768]{1,0:T(8,128)} %pick_hbm.1, s32[16,128]{1,0:T(8,128)} %bitcast.6, ...), custom_call_target="tpu_custom_call" | custom-call | tf_op jit(solution)/shard_map/modes/pallas_call | solution.py:398
  36.2 0.0 copy-done
  36.2 2.1 %legendre.1 = (f32[64,2048]{1,0:T(8,128)}, f32[64,2048]{1,0:T(8,128)}) custom-call(s32[2048]{0:T(1024)S(1)} %copy-done, f32[128,128]{1,0:T(8,128)S(1)} %get-tuple-element.7.left_ref, bf16[8,64,2048]{2,1,0:T(8,128)(2,1)S(1)} %get-tuple-element.8.a_ref, bf16[8,64,2048]{2,1,0:T(8,128)(2,1)S(1)} %get-tuple-element.9.b_ref), custom_call_target="tpu_custom_call" | custom-call | tf_op jit(solution)/shard_map/legendre/pallas_call | solution.py:447
Async XLA Ops:
  1.3 34.9 %copy-start = (s32[2048]{0:T(1024)S(1)}, s32[2048]{0:T(1024)}, u32[]{:S(2)}) copy-start(s32[2048]{0:T(1024)} %wave_ref.1) | copy-start | bytes 24580

commit v5 on v4

--- a/solution.py
+++ b/solution.py
@@ -112,6 +112,7 @@
     table,
     request_out,
     request_in,
+    taps,
     reply_out,
     reply_in,
     spectrum,
@@ -136,13 +137,13 @@
             odd = lax.rem(k, 2)
             ahead = planes // 2 + (1 - 2 * odd) * lax.div(k + 1, 2)
             base = lax.rem(plane + ahead, planes) * GROUP
-            act([base + p for p in places])
+            act(base, [base + p for p in places])
             return carry
 
         lax.fori_loop(0, planes - 1, step, 0)
-        act([plane * GROUP + p for p in places[:-1]])
-
-    def greet(others):
+        act(plane * GROUP, [plane * GROUP + p for p in places[:-1]])
+
+    def greet(base, others):
         for other in others:
             pl.semaphore_signal(barrier, 1, device_id=(other, my_lev), device_id_type=pl.DeviceIdType.MESH)
 
@@ -201,7 +202,7 @@
     )
     mine.start()
 
-    def send_request(others):
+    def send_request(base, others):
         for other in others:
             to_band(request_out.at[pl.ds(4 * other, 4)], request_in.at[pl.ds(4 * me, 4)], other, 0).start()
 
@@ -218,7 +219,7 @@
     sub = lax.broadcasted_iota(jnp.int32, (8, LANES), 0)
     lane = lax.broadcasted_iota(jnp.int32, (8, LANES), 1)
     upper = sub < 4
-    own_group = (lane >> 5) == (sub & 3)
+    group = lane >> 5
 
     def weigh(other):
         rows = [jnp.broadcast_to(request_in[pl.ds(4 * other + k, 1), :], (8, LANES)) for k in range(4)]
@@ -229,23 +230,38 @@
         for c in range(PER):
             piece = table[pick[other, pick_at + c]]
             total = jnp.where(block == c, take(piece, within), total)
-        total = total * scale
-        total = total + pltpu.roll(total, 64, 1)
-        total = total + pltpu.roll(total, 32, 1)
-        total = jnp.where(own_group, total, 0.0)
-        total = total + pltpu.roll(total, 1, 0)
-        total = total + pltpu.roll(total, 2, 0)
-        reply_out[pl.ds(2 * other, 1), :] = total[3:4]
-        reply_out[pl.ds(2 * other + 1, 1), :] = total[7:8]
-
-    def send_reply(others):
-        for other in others:
-            weigh(other)
+        return total * scale
+
+    def fold_plane(base, totals):
+        for p, total in enumerate(totals):
+            taps[pl.ds(8 * p, 8), :] = total
+        for r in range(0, 2 * GROUP, 8):
+            x, y, z = (taps[pl.ds(4 * r + a, 8, stride=4), :] for a in range(3))
+            x, y, z = (u + pltpu.roll(u, 64, 1) for u in (x, y, z))
+            x = jnp.where(lane < 64, x, z)
+            x, y = (u + pltpu.roll(u, 96, 1) for u in (x, y))
+            reply_out[pl.ds(pl.multiple_of(2 * base, 8) + r, 8), :] = jnp.where(group == 1, y, jnp.where(group == 3, 0.0, x))
+
+    def weigh_plane(base):
+        return tuple(weigh(base + p) for p in range(GROUP))
+
+    def send_reply(base, others):
         for other in others:
             to_band(reply_out.at[pl.ds(2 * other, 2)], reply_in.at[pl.ds(2 * me, 2)], other, 1).start()
 
-    each_plane(send_reply)
-    weigh(me)
+    def base_of(k):
+        ahead = planes // 2 + (1 - 2 * lax.rem(k, 2)) * lax.div(k + 1, 2)
+        return lax.rem(plane + ahead, planes) * GROUP
+
+    def reply(k, totals):
+        following = weigh_plane(base_of(k + 1))
+        fold_plane(base_of(k), totals)
+        send_reply(base_of(k), [base_of(k) + p for p in places])
+        return following
+
+    totals = lax.fori_loop(0, planes - 1, reply, weigh_plane(base_of(0)))
+    fold_plane(plane * GROUP, totals)
+    send_reply(plane * GROUP, [plane * GROUP + p for p in places[:-1]])
     mine = pltpu.make_async_copy(
         reply_out.at[pl.ds(2 * me, 2)], reply_in.at[pl.ds(2 * me, 2)], recv_sem.at[1]
     )
@@ -303,15 +319,12 @@
             packed = jnp.zeros((8, LANES), f32)
             for f in range(4):
                 packed = jnp.where(field == f, take(ordered[f], spot + 32 * b), packed)
-            rows_out[pl.ds(b * rows + 8 * h, 8), :] = packed
-
-    def row_for(other):
-        return lax.rem(other, 4) * rows + lax.div(other, 4)
+            rows_out[pl.ds(32 * h + b, 8, stride=4), :] = packed
 
     def send_row(other, levels):
         for v in levels:
             pltpu.make_async_remote_copy(
-                src_ref=rows_out.at[pl.ds(row_for(other), 1)],
+                src_ref=rows_out.at[pl.ds(other, 1)],
                 dst_ref=rows_in.at[pl.ds(my_lev * band + me, 1)],
                 send_sem=send_sem.at[2],
                 recv_sem=recv_sem.at[2],
@@ -319,14 +332,14 @@
                 device_id_type=pl.DeviceIdType.MESH,
             ).start()
 
-    def send_rows(others):
+    def send_rows(base, others):
         for other in others:
             send_row(other, my_levels)
 
     each_plane(send_rows)
     send_row(me, my_levels[:-1])
     mine = pltpu.make_async_copy(
-        rows_out.at[pl.ds(row_for(me), 1)], rows_in.at[pl.ds(my_lev * band + me, 1)], recv_sem.at[2]
+        rows_out.at[pl.ds(me, 1)], rows_in.at[pl.ds(my_lev * band + me, 1)], recv_sem.at[2]
     )
     mine.start()
     pltpu.make_async_copy(rows_in, rows_in, recv_sem.at[2]).wait()
@@ -417,6 +430,7 @@
             pltpu.VMEM((blocks, 8, BLK), f32),
             pltpu.VMEM((4 * band, LANES), f32),
             pltpu.VMEM((4 * band, LANES), f32),
+            pltpu.VMEM((8 * GROUP, LANES), f32),
             pltpu.VMEM((2 * band, LANES), f32),
             pltpu.VMEM((2 * band, LANES), f32),
             pltpu.VMEM((4 * M // LANES, LANES), f32),

time: 38.4 us -> 37.2 us (0.969)
  Pallas kernels: 37 us -> 35.8 us
    pallas_call x1, Pallas kernels: 34.9 us -> 33.7 us  [local(): pl.pallas_call(functools.partial(modes_kernel, band, lev), out_shape=(plt...]
where the time goes in v5:
time: 37.2 us; the launch traced here: 37.1 us
  Pallas kernels  35.8 us (96%)
  between operations  1.3 us (3%)
    pallas_call x1, Pallas kernels, local(): pl.pallas_call(functools.partial(modes_kernel, band, lev), out_shape=(plt...  33.7 us
    pallas_call x1, Pallas kernels, local(): pl.pallas_call(legendre_kernel, out_shape=(shape, shape), in_specs=[smem,...  2.15 us

profile of v5, /device:TPU:1, one launch (start us, length us, event | category | flops | bytes accessed | tf_op | source)
XLA Modules:
  0.0 37.1 jit_solution(17456370239646232266)
XLA Ops:
  1.3 0.0 copy-start
  1.3 33.7 %modes.1 = (f32[128,128]{1,0:T(8,128)S(1)}, bf16[8,64,2048]{2,1,0:T(8,128)(2,1)S(1)}, bf16[8,64,2048]{2,1,0:T(8,128)(2,1)S(1)}) custom-call(s32[1]{0:T(128)S(6)} %copy.14.cycle_ref, f32[768,128]{1,0:T(8,128)} %bitcast.7, f32[128,128]{1,0:T(8,128)} %bitcast.8, s32[128,128]{1,0:T(8,128)} %bitcast.9, s32[64,768]{1,0:T(8,128)} %pick_hbm.1, s32[16,128]{1,0:T(8,128)} %bitcast.6, ...), custom_call_target="tpu_custom_call" | custom-call | tf_op jit(solution)/shard_map/modes/pallas_call | solution.py:411
  35.0 0.0 copy-done
  35.0 2.1 %legendre.1 = (f32[64,2048]{1,0:T(8,128)}, f32[64,2048]{1,0:T(8,128)}) custom-call(s32[2048]{0:T(1024)S(1)} %copy-done, f32[128,128]{1,0:T(8,128)S(1)} %get-tuple-element.7.left_ref, bf16[8,64,2048]{2,1,0:T(8,128)(2,1)S(1)} %get-tuple-element.8.a_ref, bf16[8,64,2048]{2,1,0:T(8,128)(2,1)S(1)} %get-tuple-element.9.b_ref), custom_call_target="tpu_custom_call" | custom-call | tf_op jit(solution)/shard_map/legendre/pallas_call | solution.py:461
Async XLA Ops:
  1.3 33.7 %copy-start = (s32[2048]{0:T(1024)S(1)}, s32[2048]{0:T(1024)}, u32[]{:S(2)}) copy-start(s32[2048]{0:T(1024)} %wave_ref.1) | copy-start | bytes 24580

commit v6 on v5

--- a/solution.py
+++ b/solution.py
@@ -98,6 +98,7 @@
     a_hbm,
     b_hbm,
     out_ref,
+    lowest_ref,
     leg_a,
     leg_b,
     winds,
@@ -213,11 +214,18 @@
     ]
     for load in legendre_loads:
         load.start()
+    sub = lax.broadcasted_iota(jnp.int32, (8, LANES), 0)
+    lane = lax.broadcasted_iota(jnp.int32, (8, LANES), 1)
+    loads[8].wait()
+    slots = out_ref.shape[0] // (4 * lev)
+    first_slot = (me * lev + my_lev) * slots
+    near = jnp.broadcast_to(wave[pl.ds(lax.div(first_slot, LANES), 1), :], (slots, LANES))
+    own = lane == sub + lax.rem(first_slot, LANES)
+    lowest_ref[...] = jnp.broadcast_to(jnp.sum(jnp.where(own, near, 0), 1, keepdims=True), (slots, LANES))
+
     loads[3].wait()
     pltpu.make_async_copy(request_in, request_in, recv_sem.at[0]).wait()
 
-    sub = lax.broadcasted_iota(jnp.int32, (8, LANES), 0)
-    lane = lax.broadcasted_iota(jnp.int32, (8, LANES), 1)
     upper = sub < 4
     group = lane >> 5
 
@@ -266,7 +274,7 @@
         reply_out.at[pl.ds(2 * me, 2)], reply_in.at[pl.ds(2 * me, 2)], recv_sem.at[1]
     )
     mine.start()
-    for load in loads[4:]:
+    for load in loads[4:8]:
         load.wait()
     pltpu.make_async_copy(reply_in, reply_in, recv_sem.at[1]).wait()
 
@@ -369,18 +377,14 @@
     pltpu.make_async_copy(sent, sent, send_sem.at[2]).wait()
 
 
-def legendre_kernel(wave_ref, left_ref, a_ref, b_ref, div_hbm, vort_hbm, div, vort, store_sem):
-    me = lax.axis_index("band") * lax.axis_size("lev") + lax.axis_index("lev")
+def legendre_kernel(lowest_ref, left_ref, a_ref, b_ref, div_hbm, vort_hbm, div, vort, store_sem):
     owned, _, degrees = a_ref.shape
     half = left_ref.shape[0] // 2
     left = left_ref[...]
     slot = lax.broadcasted_iota(jnp.int32, left.shape, 0) % owned
     pieces = [jnp.where(slot == i, left, 0.0).astype(bf16) for i in range(owned)]
     pieces = [jnp.concatenate(pieces[i : i + 2], 1) for i in range(0, owned, 2)]
-    row = lax.broadcasted_iota(jnp.int32, (owned, WIDTH), 0)
-    lowest = jnp.zeros((owned, WIDTH), jnp.int32)
-    for i in range(owned):
-        lowest = jnp.where(row == i, wave_ref[me * owned + i], lowest)
+    lowest = jnp.concatenate([lowest_ref[...]] * (WIDTH // LANES), 1)
     stores = []
     for j in range(degrees // WIDTH):
         at = pl.ds(j * WIDTH, WIDTH)
@@ -408,15 +412,16 @@
     hbm = pl.BlockSpec(memory_space=pltpu.HBM)
     smem = pl.BlockSpec(memory_space=pltpu.SMEM)
     vmem = pl.BlockSpec(memory_space=pltpu.VMEM)
-    left, leg_a, leg_b = pl.pallas_call(
+    left, lowest, leg_a, leg_b = pl.pallas_call(
         functools.partial(modes_kernel, band, lev),
         out_shape=(
             pltpu.VMEM((4 * lev * owned, 2 * cycles), f32),
+            pltpu.VMEM((owned, LANES), jnp.int32),
             pltpu.VMEM(legendre_a.shape, bf16),
             pltpu.VMEM(legendre_b.shape, bf16),
         ),
         in_specs=[smem] + [hbm] * 11,
-        out_specs=(vmem, vmem, vmem),
+        out_specs=(vmem, vmem, vmem, vmem),
         scratch_shapes=[
             pltpu.VMEM((3 * blocks, BLK), f32),
             pltpu.VMEM((2 * band, LANES), f32),
@@ -461,7 +466,7 @@
     divergence, vorticity = pl.pallas_call(
         legendre_kernel,
         out_shape=(shape, shape),
-        in_specs=[smem, vmem, vmem, vmem],
+        in_specs=[vmem, vmem, vmem, vmem],
         out_specs=(hbm, hbm),
         scratch_shapes=[
             pltpu.VMEM(shape.shape, f32),
@@ -470,7 +475,7 @@
         ],
         compiler_params=pltpu.CompilerParams(vmem_limit_bytes=32 * 2**20),
         name="legendre",
-    )(wave_ids, left, leg_a, leg_b)
+    )(lowest, left, leg_a, leg_b)
     whole = (2, lev, owned, degrees)
     return divergence.reshape(whole), vorticity.reshape(whole)
 

time: 37.2 us -> 36.5 us (0.981)
  Pallas kernels: 35.8 us -> 35.1 us
    pallas_call x1, Pallas kernels: 2.15 us -> 1.5 us  [local(): pl.pallas_call(legendre_kernel, out_shape=(shape, shape), in_specs=[vmem,...]
where the time goes in v6:
time: 36.5 us; the launch traced here: 36.4 us
  Pallas kernels  35.1 us (96%)
  between operations  1.29 us (4%)
    pallas_call x1, Pallas kernels, local(): pl.pallas_call(functools.partial(modes_kernel, band, lev), out_shape=(plt...  33.6 us
    pallas_call x1, Pallas kernels, local(): pl.pallas_call(legendre_kernel, out_shape=(shape, shape), in_specs=[vmem,...  1.5 us

profile of v6, /device:TPU:1, one launch (start us, length us, event | category | flops | bytes accessed | tf_op | source)
XLA Modules:
  0.0 36.4 jit_solution(11090299280257065958)
XLA Ops:
  1.3 33.6 %modes.1 = (f32[128,128]{1,0:T(8,128)S(1)}, s32[8,128]{1,0:T(8,128)S(1)}, bf16[8,64,2048]{2,1,0:T(8,128)(2,1)S(1)}, bf16[8,64,2048]{2,1,0:T(8,128)(2,1)S(1)}) custom-call(s32[1]{0:T(128)S(6)} %copy.14.cycle_ref, f32[768,128]{1,0:T(8,128)} %bitcast.6, f32[128,128]{1,0:T(8,128)} %bitcast.7, s32[128,128]{1,0:T(8,128)} %bitcast.8, s32[64,768]{1,0:T(8,128)} %pick_hbm.1, ...), custom_call_target="tpu_custom_call" | custom-call | tf_op jit(solution)/shard_map/modes/pallas_call | solution.py:415
  34.9 1.5 %legendre.1 = (f32[64,2048]{1,0:T(8,128)}, f32[64,2048]{1,0:T(8,128)}) custom-call(s32[8,128]{1,0:T(8,128)S(1)} %get-tuple-element.8.lowest_ref, f32[128,128]{1,0:T(8,128)S(1)} %get-tuple-element.9.left_ref, bf16[8,64,2048]{2,1,0:T(8,128)(2,1)S(1)} %get-tuple-element.10.a_ref, bf16[8,64,2048]{2,1,0:T(8,128)(2,1)S(1)} %get-tuple-element.11.b_ref), custom_call_target="tpu_custom_call" | custom-call | tf_op jit(solution)/shard_map/legendre/pallas_call | solution.py:466

commit v7 on v6

--- a/solution.py
+++ b/solution.py
@@ -104,6 +104,8 @@
     winds,
     weight,
     column,
+    pick_window,
+    pick_rows,
     pick,
     wave,
     coef,
@@ -162,7 +164,7 @@
                 (column_hbm, column),
                 (weight_hbm, weight),
                 (winds_hbm, winds),
-                (pick_hbm.at[:, pl.ds(pl.multiple_of(window * LANES, LANES), 2 * LANES)], pick),
+                (pick_hbm.at[:, pl.ds(pl.multiple_of(window * LANES, LANES), 2 * LANES)], pick_window),
                 (coef_hbm, coef),
                 (twiddle_hbm, twiddle),
                 (inner_hbm, inner),
@@ -197,6 +199,10 @@
         part = winds[pl.ds(a * blocks, blocks), :]
         table[:, a, :] = part
         table[:, 4 + a, :] = part
+    loads[3].wait()
+    pick_rows[...] = pltpu.roll(pick_window[...], lax.rem(2 * LANES - pick_at, 2 * LANES), 1)[:, :LANES]
+    pick_load = pltpu.make_async_copy(pick_rows, pick, local_sem.at[9])
+    pick_load.start()
     pl.semaphore_wait(barrier, band - 1 + lev - 1)
     mine = pltpu.make_async_copy(
         request_out.at[pl.ds(4 * me, 4)], request_in.at[pl.ds(4 * me, 4)], recv_sem.at[0]
@@ -223,7 +229,7 @@
     own = lane == sub + lax.rem(first_slot, LANES)
     lowest_ref[...] = jnp.broadcast_to(jnp.sum(jnp.where(own, near, 0), 1, keepdims=True), (slots, LANES))
 
-    loads[3].wait()
+    pick_load.wait()
     pltpu.make_async_copy(request_in, request_in, recv_sem.at[0]).wait()
 
     upper = sub < 4
@@ -236,7 +242,7 @@
         within, block = where & (BLK - 1), where >> 7
         total = jnp.zeros((8, LANES), f32)
         for c in range(PER):
-            piece = table[pick[other, pick_at + c]]
+            piece = table[pick[other, c]]
             total = jnp.where(block == c, take(piece, within), total)
         return total * scale
 
@@ -426,7 +432,9 @@
             pltpu.VMEM((3 * blocks, BLK), f32),
             pltpu.VMEM((2 * band, LANES), f32),
             pltpu.VMEM((2 * band, LANES), jnp.int32),
-            pltpu.SMEM((band, 2 * LANES), jnp.int32),
+            pltpu.VMEM((band, 2 * LANES), jnp.int32),
+            pltpu.VMEM((band, LANES), jnp.int32),
+            pltpu.SMEM((band, LANES), jnp.int32),
             pltpu.VMEM((M // LANES, LANES), jnp.int32),
             pltpu.VMEM(coef.shape, f32),
             pltpu.VMEM(twiddle.shape, f32),
@@ -441,7 +449,7 @@
             pltpu.VMEM((4 * M // LANES, LANES), f32),
             pltpu.VMEM((band, LANES), f32),
             pltpu.VMEM((lev * band, LANES), f32),
-            pltpu.SemaphoreType.DMA((9,)),
+            pltpu.SemaphoreType.DMA((10,)),
             pltpu.SemaphoreType.DMA((3,)),
             pltpu.SemaphoreType.DMA((3,)),
             pltpu.SemaphoreType.DMA((2,)),

time: 36.5 us -> 36.1 us (0.989)
  Pallas kernels: 35.1 us -> 34.7 us
    pallas_call x1, Pallas kernels: 33.6 us -> 33.2 us  [local(): pl.pallas_call(functools.partial(modes_kernel, band, lev), out_shape=(plt...]
where the time goes in v7:
time: 36.1 us; the launch traced here: 36 us
  Pallas kernels  34.7 us (96%)
  between operations  1.29 us (4%)
    pallas_call x1, Pallas kernels, local(): pl.pallas_call(functools.partial(modes_kernel, band, lev), out_shape=(plt...  33.2 us
    pallas_call x1, Pallas kernels, local(): pl.pallas_call(legendre_kernel, out_shape=(shape, shape), in_specs=[vmem,...  1.49 us

profile of v7, /device:TPU:1, one launch (start us, length us, event | category | flops | bytes accessed | tf_op | source)
XLA Modules:
  0.0 36.0 jit_solution(17773333099437301043)
XLA Ops:
  1.3 33.2 %modes.1 = (f32[128,128]{1,0:T(8,128)S(1)}, s32[8,128]{1,0:T(8,128)S(1)}, bf16[8,64,2048]{2,1,0:T(8,128)(2,1)S(1)}, bf16[8,64,2048]{2,1,0:T(8,128)(2,1)S(1)}) custom-call(s32[1]{0:T(128)S(6)} %copy.14.cycle_ref, f32[768,128]{1,0:T(8,128)} %bitcast.6, f32[128,128]{1,0:T(8,128)} %bitcast.7, s32[128,128]{1,0:T(8,128)} %bitcast.8, s32[64,768]{1,0:T(8,128)} %pick_hbm.1, ...), custom_call_target="tpu_custom_call" | custom-call | tf_op jit(solution)/shard_map/modes/pallas_call | solution.py:421
  34.5 1.5 %legendre.1 = (f32[64,2048]{1,0:T(8,128)}, f32[64,2048]{1,0:T(8,128)}) custom-call(s32[8,128]{1,0:T(8,128)S(1)} %get-tuple-element.8.lowest_ref, f32[128,128]{1,0:T(8,128)S(1)} %get-tuple-element.9.left_ref, bf16[8,64,2048]{2,1,0:T(8,128)(2,1)S(1)} %get-tuple-element.10.a_ref, bf16[8,64,2048]{2,1,0:T(8,128)(2,1)S(1)} %get-tuple-element.11.b_ref), custom_call_target="tpu_custom_call" | custom-call | tf_op jit(solution)/shard_map/legendre/pallas_call | solution.py:474

commit v8 on v7

--- a/solution.py
+++ b/solution.py
@@ -150,7 +150,9 @@
         for other in others:
             pl.semaphore_signal(barrier, 1, device_id=(other, my_lev), device_id_type=pl.DeviceIdType.MESH)
 
-    each_plane(greet)
+    for k in range(planes):
+        base = lax.rem(plane + far_first(k, planes), planes) * GROUP
+        greet(base, [base + p for p in (places if k < planes - 1 else places[:-1])])
     for i in range(1, lev):
         other = lax.rem(my_lev + i, lev)
         pl.semaphore_signal(barrier, 1, device_id=(me, other), device_id_type=pl.DeviceIdType.MESH)
@@ -347,8 +349,9 @@
             ).start()
 
     def send_rows(base, others):
-        for other in others:
-            send_row(other, my_levels)
+        for v in my_levels:
+            for other in others:
+                send_row(other, [v])
 
     each_plane(send_rows)
     send_row(me, my_levels[:-1])

time: 36.1 us -> 35.9 us (level)
  no operation moved by 1% of the time
where the time goes in v8:
time: 35.9 us; the launch traced here: 35.8 us
  Pallas kernels  34.5 us (96%)
  between operations  1.29 us (4%)
    pallas_call x1, Pallas kernels, local(): pl.pallas_call(functools.partial(modes_kernel, band, lev), out_shape=(plt...  33 us
    pallas_call x1, Pallas kernels, local(): pl.pallas_call(legendre_kernel, out_shape=(shape, shape), in_specs=[vmem,...  1.5 us

profile of v8, /device:TPU:1, one launch (start us, length us, event | category | flops | bytes accessed | tf_op | source)
XLA Modules:
  0.0 35.8 jit_solution(5376616304183568222)
XLA Ops:
  1.3 33.0 %modes.1 = (f32[128,128]{1,0:T(8,128)S(1)}, s32[8,128]{1,0:T(8,128)S(1)}, bf16[8,64,2048]{2,1,0:T(8,128)(2,1)S(1)}, bf16[8,64,2048]{2,1,0:T(8,128)(2,1)S(1)}) custom-call(s32[1]{0:T(128)S(6)} %copy.14.cycle_ref, f32[768,128]{1,0:T(8,128)} %bitcast.6, f32[128,128]{1,0:T(8,128)} %bitcast.7, s32[128,128]{1,0:T(8,128)} %bitcast.8, s32[64,768]{1,0:T(8,128)} %pick_hbm.1, ...), custom_call_target="tpu_custom_call" | custom-call | tf_op jit(solution)/shard_map/modes/pallas_call | solution.py:424
  34.3 1.5 %legendre.1 = (f32[64,2048]{1,0:T(8,128)}, f32[64,2048]{1,0:T(8,128)}) custom-call(s32[8,128]{1,0:T(8,128)S(1)} %get-tuple-element.8.lowest_ref, f32[128,128]{1,0:T(8,128)S(1)} %get-tuple-element.9.left_ref, bf16[8,64,2048]{2,1,0:T(8,128)(2,1)S(1)} %get-tuple-element.10.a_ref, bf16[8,64,2048]{2,1,0:T(8,128)(2,1)S(1)} %get-tuple-element.11.b_ref), custom_call_target="tpu_custom_call" | custom-call | tf_op jit(solution)/shard_map/legendre/pallas_call | solution.py:477
